TPU v7x, 768 devices: a whole 4x8x12 slice. The times are simulated.
768 devices in a mesh: cuts: 8 (over x, core), scan: 96 (over y, z).
Axes of the slice: x: 4, y: 8, z: 12, core: 2. Of those that a mesh axis runs over, the one named last changes fastest.
Arguments:
- object_slices: bfloat16 [8, 2, 147456], P('cuts', None, 'scan'), may hold values from -1 to 1, as said below
- probe_wave: float32 [2, 128, 128], replicated, may hold values from -6 to 6
- intensity: float32 [192, 128, 128], P('scan'), may hold values from 0.05 to 4
- positions: int32 [192, 2], P('scan'), may hold values from 0 to 256
- counts: int32 [96], P('scan'), may hold values from 1 to 2, as said below
Outputs:
- object_gradient: float32 [8, 2, 147456], P('cuts', None, 'scan')
Inputs may be any that keep to these rules, and one draw needn't show every extreme that they name: `object_slices`: the entries (real, imaginary) of one cell form a complex number of modulus at most 1. The live slots of a device are its first counts[d] slots; some device has all 2 slots live.
All inputs are finite; a program needn't handle non-finite values.
Results may differ from a plain program's by a relative error of at most 0.0003.
Values may be sent and summed in bfloat16 or wider, within the bound.
A program may use at most 192 MiB of HBM per device.

v0:
```python
from functools import partial
import math

import jax
import jax.numpy as jnp
from jax import lax
from jax.sharding import PartitionSpec as P

NO = 384


FRESNEL = 0.5
GRAD_SCALE = 0.25


def shifted(x, axis, by):
    devices = lax.axis_size(axis)
    pairs = [(i, i + by) for i in range(devices) if 0 <= i + by < devices]
    return lax.ppermute(x, axis, pairs)


def mat_product(left_re, left_im, right_re, right_im):
    matmul = partial(jnp.dot, precision=lax.Precision.HIGHEST, preferred_element_type=jnp.float32)
    return (
        matmul(left_re, right_re) - matmul(left_im, right_im),
        matmul(left_re, right_im) + matmul(left_im, right_re),
    )


def dft_tables(window_size):
    index_row = jnp.arange(window_size, dtype=jnp.int32)
    products = index_row[:, None] * index_row[None, :] % window_size
    angles = -2.0 * math.pi / window_size * products.astype(jnp.float32)
    scaling = 1.0 / math.sqrt(window_size)
    four_re = jnp.cos(angles) * scaling
    four_im = jnp.sin(angles) * scaling
    frequency = jnp.where(index_row < window_size // 2, index_row, index_row - window_size).astype(
        jnp.float32
    )
    phases = -math.pi * FRESNEL / window_size * frequency * frequency
    half_re = jnp.cos(phases)
    half_im = jnp.sin(phases)
    scaled_re = half_re[:, None] * four_re - half_im[:, None] * four_im
    scaled_im = half_re[:, None] * four_im + half_im[:, None] * four_re
    kern_re, kern_im = mat_product(four_re.T, -four_im.T, scaled_re, scaled_im)
    return (four_re, four_im, kern_re, kern_im)


def sandwich(left_re, left_im, wave_re, wave_im, right_re, right_im):
    contract = partial(jnp.einsum, precision=lax.Precision.HIGHEST)
    mid_re = contract("ij,bjk->bik", left_re, wave_re) - contract("ij,bjk->bik", left_im, wave_im)
    mid_im = contract("ij,bjk->bik", left_re, wave_im) + contract("ij,bjk->bik", left_im, wave_re)
    out_re = contract("bij,jk->bik", mid_re, right_re) - contract("bij,jk->bik", mid_im, right_im)
    out_im = contract("bij,jk->bik", mid_re, right_im) + contract("bij,jk->bik", mid_im, right_re)
    return (out_re, out_im)


def complex_mul(a_re, a_im, b_re, b_im):
    return (a_re * b_re - a_im * b_im, a_re * b_im + a_im * b_re)


def conj_times(a_re, a_im, b_re, b_im):
    return (a_re * b_re + a_im * b_im, a_re * b_im - a_im * b_re)


def cut_windows(plane, corners, window_size):
    zero_index = jnp.zeros((), jnp.int32)
    pieces = jax.vmap(
        lambda corner: lax.dynamic_slice(
            plane, (zero_index, corner[0], corner[1]), (2, window_size, window_size)
        )
    )(corners)
    return pieces.astype(jnp.float32)


def add_windows(plane, corners, grad_re, grad_im, window_size):
    zero_index = jnp.zeros((), jnp.int32)

    def add_one(item, accumulated):
        corner = corners[item]
        anchor = (zero_index, corner[0], corner[1])
        current = lax.dynamic_slice(accumulated, anchor, (2, window_size, window_size))
        update_piece = jnp.stack([grad_re[item], grad_im[item]])
        return lax.dynamic_update_slice(accumulated, current + update_piece, anchor)

    return lax.fori_loop(0, corners.shape[0], add_one, plane)


def residual_wave(wave_re, wave_im, measured, keep_mask, four_re, four_im):
    far_re, far_im = sandwich(four_re, four_im, wave_re, wave_im, four_re.T, four_im.T)
    excess = (far_re * far_re + far_im * far_im - measured) * keep_mask[:, None, None]
    return sandwich(four_re.T, -four_im.T, excess * far_re, excess * far_im, four_re, -four_im)


def body(object_slices, probe_wave, intensity, positions, counts):
    section_count = lax.axis_size("cuts")
    section_index = lax.axis_index("cuts")
    last_section = section_count - 1
    layers_here = object_slices.shape[0]
    cell_count = object_slices.shape[2]
    slot_count = intensity.shape[0]
    window_size = probe_wave.shape[-1]
    whole_slices = lax.all_gather(object_slices, "scan", axis=2, tiled=True)
    object_field = whole_slices.reshape(layers_here, 2, NO, NO)
    four_re, four_im, kern_re, kern_im = dft_tables(window_size)
    live_mask = (jnp.arange(slot_count, dtype=jnp.int32) < counts[0]).astype(jnp.float32)
    groups = 1
    group_size = slot_count // groups
    step_count = section_count + groups - 1
    empty_wave = jnp.zeros((group_size, window_size, window_size), jnp.float32)

    def is_ready(batch_index):
        inside = (batch_index >= 0) & (batch_index < groups)
        return inside

    def forward_step(step_now, carry):
        batch_index = step_now - section_index
        first_row = jnp.clip(batch_index, 0, groups - 1) * group_size

        def forward_do_work(operands):
            recv_re, recv_im, saved_re, saved_im, chi_re, chi_im = operands
            wave_re = jnp.where(section_index == 0, probe_wave[0][None], recv_re)
            wave_im = jnp.where(section_index == 0, probe_wave[1][None], recv_im)
            window = cut_windows(object_field[0], positions, window_size)
            saved_re = saved_re.at[0].set(wave_re)
            saved_im = saved_im.at[0].set(wave_im)
            trans_re, trans_im = complex_mul(wave_re, wave_im, window[:, 0], window[:, 1])
            wave_re, wave_im = sandwich(kern_re, kern_im, trans_re, trans_im, kern_re.T, kern_im.T)

            def far_field(waves):
                return residual_wave(waves[0], waves[1], intensity, live_mask, four_re, four_im)

            def no_field(waves):
                return (empty_wave, empty_wave)

            res_re, res_im = lax.cond(
                section_index == last_section, far_field, no_field, (wave_re, wave_im)
            )
            chi_re = lax.dynamic_update_slice_in_dim(chi_re, res_re, first_row, 0)
            chi_im = lax.dynamic_update_slice_in_dim(chi_im, res_im, first_row, 0)
            return (wave_re, wave_im, saved_re, saved_im, chi_re, chi_im)

        def forward_pass_on(operands):
            return (empty_wave, empty_wave) + tuple(operands[2:])

        result_set = lax.cond(is_ready(batch_index), forward_do_work, forward_pass_on, carry)
        sent_re, sent_im = shifted((result_set[0], result_set[1]), "cuts", 1)
        return (sent_re, sent_im) + tuple(result_set[2:])

    store_shape = (layers_here, slot_count, window_size, window_size)
    chi_shape = (slot_count, window_size, window_size)
    start_carry = (
        empty_wave,
        empty_wave,
        jnp.zeros(store_shape, jnp.float32),
        jnp.zeros(store_shape, jnp.float32),
        jnp.zeros(chi_shape, jnp.float32),
        jnp.zeros(chi_shape, jnp.float32),
    )
    forward_out = lax.fori_loop(0, step_count, forward_step, start_carry)
    saved_re, saved_im, chi_store_re, chi_store_im = (
        forward_out[2],
        forward_out[3],
        forward_out[4],
        forward_out[5],
    )

    def backward_step(step_now, carry):
        batch_index = step_now - (last_section - section_index)
        first_row = jnp.clip(batch_index, 0, groups - 1) * group_size

        def backward_do_work(operands):
            recv_re, recv_im, planes = operands
            planes = list(planes)
            chi_re = jnp.where(section_index == last_section, chi_store_re, recv_re)
            chi_im = jnp.where(section_index == last_section, chi_store_im, recv_im)
            for layer in reversed(range(layers_here)):
                window = cut_windows(object_field[layer], positions, window_size)
                incoming_re = saved_re[layer]
                incoming_im = saved_im[layer]
                back_re, back_im = sandwich(
                    kern_re.T, -kern_im.T, chi_re, chi_im, kern_re, -kern_im
                )
                grad_re, grad_im = conj_times(incoming_re, incoming_im, back_re, back_im)
                planes[layer] = add_windows(planes[layer], positions, grad_re, grad_im, window_size)
                chi_re, chi_im = conj_times(window[:, 0], window[:, 1], back_re, back_im)
            return (chi_re, chi_im, tuple(planes))

        def backward_pass_on(operands):
            return (empty_wave, empty_wave, operands[2])

        result_set = lax.cond(is_ready(batch_index), backward_do_work, backward_pass_on, carry)
        sent_re, sent_im = shifted((result_set[0], result_set[1]), "cuts", -1)
        return (sent_re, sent_im, result_set[2])

    start_grad = tuple((jnp.zeros((2, NO, NO), jnp.float32) for layer in range(layers_here)))
    backward_out = lax.fori_loop(0, step_count, backward_step, (empty_wave, empty_wave, start_grad))
    flat_grad = jnp.stack(backward_out[2]).reshape(layers_here, 2, NO * NO)
    summed = lax.psum(flat_grad, "scan")
    own_part = lax.dynamic_slice_in_dim(summed, lax.axis_index("scan") * cell_count, cell_count, 2)
    return own_part * GRAD_SCALE


def solution(mesh):
    in_specs = (P("cuts", None, "scan"), P(), P("scan", None, None), P("scan", None), P("scan"))
    out_specs = P("cuts", None, "scan")
    return jax.shard_map(body, mesh=mesh, in_specs=in_specs, out_specs=out_specs, check_vma=False)
```

profile of v0, /device:TPU:1, one launch (start us, length us, event | category | flops | bytes accessed | tf_op | source)
XLA Modules:
  0.0 710.0 jit_solution(6937123743969192396)
XLA Ops:
  8.7 66.0 %all_gather.3 = bf16[1,2,147456]{2,1,0:T(2,128)(2,1)S(1)} all-gather(bf16[1,2,1536]{2,1,0:T(2,128)(2,1)S(1)} %copy-done.4), channel_id=1, replica_groups=mesh['cuts'=8,'scan'=96] {'scan'}, dimensions={2}, use_global_device_ids=true | all-gather | bytes 595968 | tf_op jit(solution)/shard_map/all_gather | solution.py:103
  76.2 142.9 %while.67 = (s32[]{:T(128)}, f32[2,128,128]{2,1,0:T(8,128)S(1)}, f32[2,128,128]{2,1,0:T(8,128)S(1)}, f32[1,2,128,128]{3,2,1,0:T(8,128)S(1)}, f32[1,2,128,128]{3,...) while((s32[]{:T(128)}, f32[2,128,128]{2,1,0:T(8,128)S(1)}, ...), condition=%wide.region_5.6_spmd.clone.clone, body=%wide.region_0.5_spmd.clone.clone.sunk | while | flops 1209237504 | bytes 14549956 | solution.py:160
  78.2 22.0 %collective-permute-start = (f32[2,128,128]{2,1,0:T(8,128)}, f32[2,128,128]{2,1,0:T(8,128)S(1)}, u32[]{:S(2)}, u32[]{:S(2)}) collective-permute-start(f32[2,128,128]{2,1,0:T(8,128)} %get-tuple-element.1533), channel_id=1, source_target_pairs={{0,96},{96,192},{192,288},{288,384},{384,480},{480,576},{576,672},... | collective-permute-start | bytes 393224 | tf_op jit(solution)/shard_map/while/body/eval_jaxpr/ppermute | solution.py:19
  102.2 6.7 collective-permute-done
  110.8 10.6 %conditional.9 = (f32[2,128,128]{2,1,0:T(8,128)}, f32[2,128,128]{2,1,0:T(8,128)}, f32[1,2,128,128]{3,2,1,0:T(8,128)S(1)}, f32[1,2,128,128]{3,2,1,0:T(8,128)S(1)}...) conditional(s32[]{:T(128)} %convert_element_type.173, (f32[1,2,128,128]{3,2,1,0:T(8,128)S(1)}, ...), branch_computations={%region_1.1_spmd, %region_2.4_spmd.clone} | conditional | flops 1209008128 | bytes 13369865 | solution.py:146
  111.6 4.0 while.65
  129.6 13.5 %collective-permute-start = (f32[2,128,128]{2,1,0:T(8,128)}, f32[2,128,128]{2,1,0:T(8,128)S(1)}, u32[]{:S(2)}, u32[]{:S(2)}) collective-permute-start(f32[2,128,128]{2,1,0:T(8,128)} %get-tuple-element.1533), channel_id=1, source_target_pairs={{0,96},{96,192},{192,288},{288,384},{384,480},{480,576},{576,672},... | collective-permute-start | bytes 393224 | tf_op jit(solution)/shard_map/while/body/eval_jaxpr/ppermute | solution.py:19
  149.3 4.2 collective-permute-start
  153.6 8.1 %collective-permute-start.1 = (f32[2,128,128]{2,1,0:T(8,128)}, f32[2,128,128]{2,1,0:T(8,128)S(1)}, u32[]{:S(2)}, u32[]{:S(2)}) collective-permute-start(f32[2,128,128]{2,1,0:T(8,128)} %get-tuple-element.1534), channel_id=1, source_target_pairs={{0,96},{96,192},{192,288},{288,384},{384,480},{480,576},{576,672},... | collective-permute-start | bytes 393224 | tf_op jit(solution)/shard_map/while/body/eval_jaxpr/ppermute | solution.py:19
  161.7 2.2 collective-permute-done.1
  166.0 4.2 collective-permute-start
  176.5 10.1 %collective-permute-start = (f32[2,128,128]{2,1,0:T(8,128)}, f32[2,128,128]{2,1,0:T(8,128)S(1)}, u32[]{:S(2)}, u32[]{:S(2)}) collective-permute-start(f32[2,128,128]{2,1,0:T(8,128)} %get-tuple-element.1533), channel_id=1, source_target_pairs={{0,96},{96,192},{192,288},{288,384},{384,480},{480,576},{576,672},... | collective-permute-start | bytes 393224 | tf_op jit(solution)/shard_map/while/body/eval_jaxpr/ppermute | solution.py:19
  186.6 3.0 collective-permute-start.1
  189.6 2.2 collective-permute-done.1
  193.9 4.2 collective-permute-start
  198.2 8.1 %collective-permute-start.1 = (f32[2,128,128]{2,1,0:T(8,128)}, f32[2,128,128]{2,1,0:T(8,128)S(1)}, u32[]{:S(2)}, u32[]{:S(2)}) collective-permute-start(f32[2,128,128]{2,1,0:T(8,128)} %get-tuple-element.1534), channel_id=1, source_target_pairs={{0,96},{96,192},{192,288},{288,384},{384,480},{480,576},{576,672},... | collective-permute-start | bytes 393224 | tf_op jit(solution)/shard_map/while/body/eval_jaxpr/ppermute | solution.py:19
  210.6 4.2 collective-permute-start
  221.2 254.6 %while.66 = (s32[]{:T(128)}, f32[2,128,128]{2,1,0:T(8,128)S(1)}, f32[2,128,128]{2,1,0:T(8,128)S(1)}, f32[2,384,384]{2,1,0:T(8,128)S(1)}, s32[]{:T(128)}, /*index...) while((s32[]{:T(128)}, f32[2,128,128]{2,1,0:T(8,128)S(1)}, ...), condition=%wide.region_11.12_spmd, body=%wide.region_6.11_spmd.sunk | while | flops 403505152 | bytes 8913846 | solution.py:197
  226.6 8.1 %collective-permute-done.2 = f32[2,128,128]{2,1,0:T(8,128)S(1)} collective-permute-done((f32[2,128,128]{2,1,0:T(8,128)}, f32[2,128,128]{2,1,0:T(8,128)S(1)}, u32[]{:S(2)}, u32[]{:S(2)}) %collective-permute-start.2) | collective-permute-done | bytes 131104 | tf_op jit(solution)/shard_map/while/body/eval_jaxpr/ppermute | solution.py:19
  241.7 2.6 collective-permute-done.2
  251.5 2.6 collective-permute-done.2
  261.2 14.5 %collective-permute-done.2 = f32[2,128,128]{2,1,0:T(8,128)S(1)} collective-permute-done((f32[2,128,128]{2,1,0:T(8,128)}, f32[2,128,128]{2,1,0:T(8,128)S(1)}, u32[]{:S(2)}, u32[]{:S(2)}) %collective-permute-start.2) | collective-permute-done | bytes 131104 | tf_op jit(solution)/shard_map/while/body/eval_jaxpr/ppermute | solution.py:19
  282.7 3.2 collective-permute-done.2
  293.1 122.0 %collective-permute-done.2 = f32[2,128,128]{2,1,0:T(8,128)S(1)} collective-permute-done((f32[2,128,128]{2,1,0:T(8,128)}, f32[2,128,128]{2,1,0:T(8,128)S(1)}, u32[]{:S(2)}, u32[]{:S(2)}) %collective-permute-start.2) | collective-permute-done | bytes 131104 | tf_op jit(solution)/shard_map/while/body/eval_jaxpr/ppermute | solution.py:19
  417.0 22.5 %conditional.8 = (f32[2,128,128]{2,1,0:T(8,128)}, f32[2,128,128]{2,1,0:T(8,128)}, f32[2,384,384]{2,1,0:T(8,128)S(1)}) conditional(s32[]{:T(128)} %convert_element_type.170, f32[2,384,384]{2,1,0:T(8,128)S(1)} %get-tuple-element.1709, (bf16[1,2,147456]{2,1,0:T(2,128)(2,1)S(1)}, s32[2,2]{1,0:T(2,128)S(1)}, s32[]{:T(128)}, f32[2,128,128]{1,2,0:T(8,128)S(1)}, ...), branch_computations={%region_7.7_spmd, %region_8.10_spmd} | conditional | flops 403505152 | bytes 7864907 | solution.py:192
  419.7 4.1 while.64
  425.8 13.7 %while.63 = (s32[]{:T(128)}, f32[2,384,384]{2,1,0:T(8,128)S(1)}, s32[2,2]{1,0:T(2,128)S(1)}, f32[2,128,128]{2,1,0:T(8,128)S(1)}, f32[2,128,128]{2,1,0:T(8,128)S(1)}, /*index=5*/s32[]{:T(128)}, s32[]{:T(128)}, s32[]{:T(128)}) while((s32[]{:T(128)}, f32[2,384,384]{2,1,0:T(8,128)S(1)}, s32[2,2]{1,0:T(2,128)S(1)}, f32[2,128,128]{2,1,0:T(8,128)S(1)}, ...), condition=%wide.region_10.9_spmd, body=%wide.region_9.8_spmd.sunk | while | flops 65544 | bytes 917717 | solution.py:86
  437.0 2.5 dynamic_update_slice.10
  443.4 2.6 collective-permute-done.2
  449.3 20.1 %collective-permute-start.2 = (f32[2,128,128]{2,1,0:T(8,128)}, f32[2,128,128]{2,1,0:T(8,128)S(1)}, u32[]{:S(2)}, u32[]{:S(2)}) collective-permute-start(f32[2,128,128]{2,1,0:T(8,128)} %get-tuple-element.1515), channel_id=1, source_target_pairs={{96,0},{192,96},{288,192},{384,288},{480,384},{576,480},{672,576},... | collective-permute-start | bytes 393224 | tf_op jit(solution)/shard_map/while/body/eval_jaxpr/ppermute | solution.py:19
  471.3 4.6 collective-permute-done.3
  477.7 224.2 %all-reduce.2.cloned.1.call-done = f32[1,2,147456]{2,1,0:T(2,128)} async-done(((f32[1,2,147456]{2,1,0:T(2,128)}), f32[1,2,147456]{2,1,0:T(2,128)}) %all-reduce.2.cloned.1.call-update) | async-done | bytes 1179664 | tf_op jit(solution)/shard_map/psum | solution.py:199
  (195 shorter events, 141.7 us)
Async XLA Ops:
  6.5 695.3 %all-reduce.2.cloned.1.call-start = ((), (), s32[]{:S(2)}) async-start(), calls=%async_computation | async-start | bytes 2359296 | tf_op jit(solution)/shard_map/psum | solution.py:199
  78.2 30.6 %collective-permute-start = (f32[2,128,128]{2,1,0:T(8,128)}, f32[2,128,128]{2,1,0:T(8,128)S(1)}, u32[]{:S(2)}, u32[]{:S(2)}) collective-permute-start(f32[2,128,128]{2,1,0:T(8,128)} %get-tuple-element.1533), channel_id=1, source_target_pairs={{0,96},{96,192},{192,288},{288,384},{384,480},{480,576},{576,672},... | collective-permute-start | bytes 393224 | tf_op jit(solution)/shard_map/while/body/eval_jaxpr/ppermute | solution.py:19
  100.2 9.9 %collective-permute-start.1 = (f32[2,128,128]{2,1,0:T(8,128)}, f32[2,128,128]{2,1,0:T(8,128)S(1)}, u32[]{:S(2)}, u32[]{:S(2)}) collective-permute-start(f32[2,128,128]{2,1,0:T(8,128)} %get-tuple-element.1534), channel_id=1, source_target_pairs={{0,96},{96,192},{192,288},{288,384},{384,480},{480,576},{576,672},... | collective-permute-start | bytes 393224 | tf_op jit(solution)/shard_map/while/body/eval_jaxpr/ppermute | solution.py:19
  123.4 4.2 collective-permute-start.1
  129.6 15.8 %collective-permute-start = (f32[2,128,128]{2,1,0:T(8,128)}, f32[2,128,128]{2,1,0:T(8,128)S(1)}, u32[]{:S(2)}, u32[]{:S(2)}) collective-permute-start(f32[2,128,128]{2,1,0:T(8,128)} %get-tuple-element.1533), channel_id=1, source_target_pairs={{0,96},{96,192},{192,288},{288,384},{384,480},{480,576},{576,672},... | collective-permute-start | bytes 393224 | tf_op jit(solution)/shard_map/while/body/eval_jaxpr/ppermute | solution.py:19
  143.1 4.2 collective-permute-start.1
  149.3 12.4 %collective-permute-start = (f32[2,128,128]{2,1,0:T(8,128)}, f32[2,128,128]{2,1,0:T(8,128)S(1)}, u32[]{:S(2)}, u32[]{:S(2)}) collective-permute-start(f32[2,128,128]{2,1,0:T(8,128)} %get-tuple-element.1533), channel_id=1, source_target_pairs={{0,96},{96,192},{192,288},{288,384},{384,480},{480,576},{576,672},... | collective-permute-start | bytes 393224 | tf_op jit(solution)/shard_map/while/body/eval_jaxpr/ppermute | solution.py:19
  153.6 10.4 %collective-permute-start.1 = (f32[2,128,128]{2,1,0:T(8,128)}, f32[2,128,128]{2,1,0:T(8,128)S(1)}, u32[]{:S(2)}, u32[]{:S(2)}) collective-permute-start(f32[2,128,128]{2,1,0:T(8,128)} %get-tuple-element.1534), channel_id=1, source_target_pairs={{0,96},{96,192},{192,288},{288,384},{384,480},{480,576},{576,672},... | collective-permute-start | bytes 393224 | tf_op jit(solution)/shard_map/while/body/eval_jaxpr/ppermute | solution.py:19
  166.0 6.5 collective-permute-start
  170.3 4.2 collective-permute-start.1
  176.5 13.1 %collective-permute-start = (f32[2,128,128]{2,1,0:T(8,128)}, f32[2,128,128]{2,1,0:T(8,128)S(1)}, u32[]{:S(2)}, u32[]{:S(2)}) collective-permute-start(f32[2,128,128]{2,1,0:T(8,128)} %get-tuple-element.1533), channel_id=1, source_target_pairs={{0,96},{96,192},{192,288},{288,384},{384,480},{480,576},{576,672},... | collective-permute-start | bytes 393224 | tf_op jit(solution)/shard_map/while/body/eval_jaxpr/ppermute | solution.py:19
  186.6 5.2 collective-permute-start.1
  193.9 12.4 %collective-permute-start = (f32[2,128,128]{2,1,0:T(8,128)}, f32[2,128,128]{2,1,0:T(8,128)S(1)}, u32[]{:S(2)}, u32[]{:S(2)}) collective-permute-start(f32[2,128,128]{2,1,0:T(8,128)} %get-tuple-element.1533), channel_id=1, source_target_pairs={{0,96},{96,192},{192,288},{288,384},{384,480},{480,576},{576,672},... | collective-permute-start | bytes 393224 | tf_op jit(solution)/shard_map/while/body/eval_jaxpr/ppermute | solution.py:19
  198.2 10.4 %collective-permute-start.1 = (f32[2,128,128]{2,1,0:T(8,128)}, f32[2,128,128]{2,1,0:T(8,128)S(1)}, u32[]{:S(2)}, u32[]{:S(2)}) collective-permute-start(f32[2,128,128]{2,1,0:T(8,128)} %get-tuple-element.1534), channel_id=1, source_target_pairs={{0,96},{96,192},{192,288},{288,384},{384,480},{480,576},{576,672},... | collective-permute-start | bytes 393224 | tf_op jit(solution)/shard_map/while/body/eval_jaxpr/ppermute | solution.py:19
  210.6 6.5 collective-permute-start
  214.9 4.2 collective-permute-start.1
  222.7 11.9 %collective-permute-start.2 = (f32[2,128,128]{2,1,0:T(8,128)}, f32[2,128,128]{2,1,0:T(8,128)S(1)}, u32[]{:S(2)}, u32[]{:S(2)}) collective-permute-start(f32[2,128,128]{2,1,0:T(8,128)} %get-tuple-element.1515), channel_id=1, source_target_pairs={{96,0},{192,96},{288,192},{384,288},{480,384},{576,480},{672,576},... | collective-permute-start | bytes 393224 | tf_op jit(solution)/shard_map/while/body/eval_jaxpr/ppermute | solution.py:19
  224.7 11.9 %collective-permute-start.3 = (f32[2,128,128]{2,1,0:T(8,128)}, f32[2,128,128]{2,1,0:T(8,128)S(1)}, u32[]{:S(2)}, u32[]{:S(2)}) collective-permute-start(f32[2,128,128]{2,1,0:T(8,128)} %get-tuple-element.1516), channel_id=1, source_target_pairs={{96,0},{192,96},{288,192},{384,288},{480,384},{576,480},{672,576},... | collective-permute-start | bytes 393224 | tf_op jit(solution)/shard_map/while/body/eval_jaxpr/ppermute | solution.py:19
  237.9 6.5 collective-permute-start.2
  239.8 6.5 collective-permute-start.3
  247.6 6.5 collective-permute-start.2
  249.5 6.5 collective-permute-start.3
  257.3 18.3 %collective-permute-start.2 = (f32[2,128,128]{2,1,0:T(8,128)}, f32[2,128,128]{2,1,0:T(8,128)S(1)}, u32[]{:S(2)}, u32[]{:S(2)}) collective-permute-start(f32[2,128,128]{2,1,0:T(8,128)} %get-tuple-element.1515), channel_id=1, source_target_pairs={{96,0},{192,96},{288,192},{384,288},{480,384},{576,480},{672,576},... | collective-permute-start | bytes 393224 | tf_op jit(solution)/shard_map/while/body/eval_jaxpr/ppermute | solution.py:19
  259.3 18.3 %collective-permute-start.3 = (f32[2,128,128]{2,1,0:T(8,128)}, f32[2,128,128]{2,1,0:T(8,128)S(1)}, u32[]{:S(2)}, u32[]{:S(2)}) collective-permute-start(f32[2,128,128]{2,1,0:T(8,128)} %get-tuple-element.1516), channel_id=1, source_target_pairs={{96,0},{192,96},{288,192},{384,288},{480,384},{576,480},{672,576},... | collective-permute-start | bytes 393224 | tf_op jit(solution)/shard_map/while/body/eval_jaxpr/ppermute | solution.py:19
  278.9 7.1 collective-permute-start.2
  280.8 7.1 %collective-permute-start.3 = (f32[2,128,128]{2,1,0:T(8,128)}, f32[2,128,128]{2,1,0:T(8,128)S(1)}, u32[]{:S(2)}, u32[]{:S(2)}) collective-permute-start(f32[2,128,128]{2,1,0:T(8,128)} %get-tuple-element.1516), channel_id=1, source_target_pairs={{96,0},{192,96},{288,192},{384,288},{480,384},{576,480},{672,576},... | collective-permute-start | bytes 393224 | tf_op jit(solution)/shard_map/while/body/eval_jaxpr/ppermute | solution.py:19
  289.2 125.9 %collective-permute-start.2 = (f32[2,128,128]{2,1,0:T(8,128)}, f32[2,128,128]{2,1,0:T(8,128)S(1)}, u32[]{:S(2)}, u32[]{:S(2)}) collective-permute-start(f32[2,128,128]{2,1,0:T(8,128)} %get-tuple-element.1515), channel_id=1, source_target_pairs={{96,0},{192,96},{288,192},{384,288},{480,384},{576,480},{672,576},... | collective-permute-start | bytes 393224 | tf_op jit(solution)/shard_map/while/body/eval_jaxpr/ppermute | solution.py:19
  291.1 125.9 %collective-permute-start.3 = (f32[2,128,128]{2,1,0:T(8,128)}, f32[2,128,128]{2,1,0:T(8,128)S(1)}, u32[]{:S(2)}, u32[]{:S(2)}) collective-permute-start(f32[2,128,128]{2,1,0:T(8,128)} %get-tuple-element.1516), channel_id=1, source_target_pairs={{96,0},{192,96},{288,192},{384,288},{480,384},{576,480},{672,576},... | collective-permute-start | bytes 393224 | tf_op jit(solution)/shard_map/while/body/eval_jaxpr/ppermute | solution.py:19
  439.5 6.5 collective-permute-start.2
  441.4 6.5 collective-permute-start.3
  449.3 22.0 %collective-permute-start.2 = (f32[2,128,128]{2,1,0:T(8,128)}, f32[2,128,128]{2,1,0:T(8,128)S(1)}, u32[]{:S(2)}, u32[]{:S(2)}) collective-permute-start(f32[2,128,128]{2,1,0:T(8,128)} %get-tuple-element.1515), channel_id=1, source_target_pairs={{96,0},{192,96},{288,192},{384,288},{480,384},{576,480},{672,576},... | collective-permute-start | bytes 393224 | tf_op jit(solution)/shard_map/while/body/eval_jaxpr/ppermute | solution.py:19
  469.3 6.5 collective-permute-start.3
  (6 other events, 212.2 us)
Sparse Core Ops, SparseCore 0:
  477.8 224.0 all-reduce.1
where the time goes:
time: 717 us; the launch traced here: 710 us
  waiting for transfers between devices  422 us (59%)
  starting transfers between devices  142 us (20%)
  blocking collectives  66 us (9%)
  local copies, waits for them, and re-layouts  39.5 us (6%)
  between operations  13.6 us (2%)
  matrix products  10.7 us (1%)
  loops' own time  8.68 us (1%)
  other arithmetic  7.93 us (1%)
    psum x1, waiting for transfers between devices, body(): summed = lax.psum(flat_grad, 'scan')  224 us
    ppermute x32, waiting for transfers between devices, shifted(): return lax.ppermute(x, axis, pairs)  197 us
    ppermute x32, starting transfers between devices, shifted(): return lax.ppermute(x, axis, pairs)  142 us
    all_gather x1, blocking collectives, body(): whole_slices = lax.all_gather(object_slices, 'scan', axis=2, tiled=True)  66 us
    another operation x50, local copies, waits for them, and re-layouts  21.4 us
  transfers between devices with their start and end apart: 33, of which 29 were waited for; matrix products, arithmetic and copies ran while one was open for 0% of the time, Pallas kernels for 0%

commit v1 on v0

v1 whole, which is shorter than its diff:
```python
import functools

import jax
import jax.numpy as jnp
import ml_dtypes
import numpy as np
from jax import lax
from jax.experimental import pallas as pl
from jax.experimental.pallas import tpu as pltpu
from jax.sharding import PartitionSpec as P

WIN = 128
FRESNEL = 0.5
GRAD_SCALE = 0.25
NZ = 12
F32 = jnp.float32
BF16 = jnp.bfloat16
MESH = pl.DeviceIdType.MESH


def row_order():
    rho = np.arange(WIN)
    q, k, m, rr = rho // 32, (rho // 8) % 4, (rho // 4) % 2, rho % 4
    return 32 * k + 16 * (q // 2) + 8 * m + 4 * (q % 2) + rr


def split_table(mat):
    hi = mat.astype(ml_dtypes.bfloat16)
    lo = (mat - hi.astype(np.float64)).astype(ml_dtypes.bfloat16)
    return np.stack([hi, lo])


def tables():
    k = np.arange(WIN)
    four = np.exp(-2j * np.pi * ((k[:, None] * k[None, :]) % WIN) / WIN) / np.sqrt(WIN)
    freq = np.where(k < WIN // 2, k, k - WIN).astype(np.float64)
    half = np.exp(-1j * np.pi * FRESNEL * freq * freq / WIN)
    kern = np.conj(four.T) @ (half[:, None] * four)
    order = row_order()

    def right(mat):
        return split_table(np.block([[mat.real, mat.imag], [-mat.imag, mat.real]]))

    def left(mat):
        return split_table(np.block([[mat.real, -mat.imag], [mat.imag, mat.real]]))

    return np.stack(
        [
            right(kern),
            left(kern[order][:, order]),
            right(four),
            left(four[:, order]),
            left(four[order]),
        ]
    )


def dot(a, b):
    return jnp.dot(a, b, preferred_element_type=F32)


def split(x):
    hi = x.astype(BF16)
    return hi, (x - hi.astype(F32)).astype(BF16)


def sandwich(x, right, left):
    hi, lo = split(x)
    both = dot(jnp.concatenate([hi, lo], 0), right[0])
    mid = both[:WIN] + both[WIN:] + dot(hi, right[1])
    mid = jnp.concatenate([mid[:, :WIN], mid[:, WIN:]], 0)
    hi, lo = split(mid)
    both = dot(left[0], jnp.concatenate([hi, lo], 1))
    out = both[:, :WIN] + both[:, WIN:] + dot(left[1], hi)
    return jnp.concatenate([out[:WIN], out[WIN:]], 1)


def complex_mul(x, w):
    x_re, x_im, w_re, w_im = x[:, :WIN], x[:, WIN:], w[:, :WIN], w[:, WIN:]
    return jnp.concatenate([x_re * w_re - x_im * w_im, x_re * w_im + x_im * w_re], 1)


def rolled_probe(probe_ref, row_at, col_at):
    shape = (WIN, WIN)
    rho = lax.broadcasted_iota(jnp.int32, shape, 0)
    lane = lax.broadcasted_iota(jnp.int32, shape, 1)
    t = (
        32 * ((rho >> 3) & 3)
        + 16 * ((rho >> 6) & 1)
        + 8 * ((rho >> 2) & 1)
        + 4 * ((rho >> 5) & 1)
        + (rho & 3)
    )
    rows = (((t - lane - row_at) & (WIN - 1)) == 0).astype(F32).astype(BF16)
    cols = (((lane - rho - col_at) & (WIN - 1)) == 0).astype(F32).astype(BF16)
    halves = []
    for plane in range(2):
        rest = probe_ref[plane]
        total = jnp.zeros(shape, F32)
        for _ in range(3):
            part = rest.astype(BF16)
            rest = rest - part.astype(F32)
            total = total + dot(dot(rows, part).astype(BF16), cols)
        halves.append(total)
    return jnp.concatenate(halves, 1)


def swap_halves(x):
    return jnp.concatenate([x[..., 4:8, :], x[..., 0:4, :]], -2)


def kernel(
    obj_ref, aux_ref, probe_ref, inten_ref, tab_ref,
    out_ref,
    cells, cells_f32, aux_all, pieces, win, psis, wave, esend, erecv, fsend, frecv,
    a_send, a_recv, p_send, p_recv, b_send, b_recv, c_send, c_recv, e_send, e_recv, f_send, f_recv, local_sem,
):
    cut = lax.axis_index("cuts")
    me = lax.axis_index("scan")
    x, core = cut // 2, cut % 2
    y, z = me // NZ, me % NZ
    bit_a = z % 2
    bit_b = (y + z // 4) % 2
    q = 2 * bit_b + bit_a
    my_slot = (me // 32) * 8 + ((me // 8) % 4) * 2 + (me // 2) % 2

    def owner(slot):
        return (slot // 8) * 32 + ((slot // 2) % 4) * 8 + 4 * bit_b + 2 * (slot % 2) + bit_a

    def mate(dq):
        y_to = y + 1 - 2 * (y % 2) if dq >= 2 else y
        z_to = z + 1 - 2 * (z % 2) if dq % 2 else z
        return y_to * NZ + z_to

    def mate_class(dq):
        b_to = 1 - bit_b if dq >= 2 else bit_b
        a_to = 1 - bit_a if dq % 2 else bit_a
        return 2 * b_to + a_to

    def core_of(dj):
        return 1 - core if dj else core

    def cut_of(dj):
        return 2 * x + core_of(dj)

    barrier = pltpu.get_barrier_semaphore()

    def greet(d, carry):
        to = owner(lax.rem(my_slot + d, 24))
        pl.semaphore_signal(barrier, inc=1, device_id={"cuts": cut, "scan": to}, device_id_type=MESH)
        return carry

    lax.fori_loop(1, 24, greet, 0)
    for dj in range(2):
        for dq in range(4):
            if dj or dq:
                pl.semaphore_signal(
                    barrier, inc=1, device_id={"cuts": cut_of(dj), "scan": mate(dq)}, device_id_type=MESH
                )
    for d in range(1, 4):
        to = 2 * lax.rem(x + d, 4) + core
        pl.semaphore_signal(barrier, inc=1, device_id={"cuts": to, "scan": me}, device_id_type=MESH)
    pl.semaphore_wait(barrier, 33)

    def aux_copy(dq):
        return pltpu.make_async_remote_copy(
            src_ref=aux_ref, dst_ref=aux_all.at[q], send_sem=p_send.at[dq], recv_sem=p_recv.at[dq],
            device_id={"cuts": cut, "scan": mate(dq)}, device_id_type=MESH,
        )

    def cell_copy(d):
        return pltpu.make_async_remote_copy(
            src_ref=obj_ref, dst_ref=cells.at[my_slot], send_sem=a_send.at[d], recv_sem=a_recv.at[d],
            device_id={"cuts": cut, "scan": owner(lax.rem(my_slot + d, 24))}, device_id_type=MESH,
        )

    for dq in range(1, 4):
        aux_copy(dq).start()

    def start_cells(d, carry):
        cell_copy(d).start()
        return carry

    lax.fori_loop(1, 24, start_cells, 0)
    aux_all[q] = aux_ref[...]
    cells[my_slot] = obj_ref[...]

    row_at = aux_ref[pl.ds(2 * core, 1), :].astype(jnp.int32)
    col_at = aux_ref[pl.ds(2 * core + 1, 1), :].astype(jnp.int32)
    wave[...] = rolled_probe(probe_ref, row_at, col_at)

    for dq in range(1, 4):
        aux_copy(dq).wait()

    def wait_cells(d, carry):
        cell_copy(d).wait()
        return carry

    lax.fori_loop(1, 24, wait_cells, 0)
    cells_f32[...] = cells[...].astype(F32)

    tile = (8, WIN)
    sub = lax.broadcasted_iota(jnp.int32, tile, 0)
    lane = lax.broadcasted_iota(jnp.int32, tile, 1)
    low = sub < 4

    def pick(n, carry):
        qt, j = n // 2, n % 2
        a = aux_all[qt, pl.ds(2 * j, 1), :].astype(jnp.int32)
        b = aux_all[qt, pl.ds(2 * j + 1, 1), :].astype(jnp.int32)
        row0 = (sub & 3) + (16 * bit_b + 4 * bit_a) - a
        in_c0 = ((lane - b) & -WIN) == 0
        in_c1 = ((lane + WIN - b) & -WIN) == 0
        for k in range(4):
            halves = []
            for m in range(2):
                cand = []
                for third in range(3):
                    blk = third * 8 + k * 2 + m
                    c0, c1, c2 = (cells_f32[blk, 8 * c : 8 * c + 8, :] for c in range(3))
                    cand.append(jnp.where(in_c0, c0, jnp.where(in_c1, c1, c2)))
                row = row0 + (32 * k + 8 * m)
                in_r0 = (row & -WIN) == 0
                in_r1 = ((row + WIN) & -WIN) == 0
                halves.append(jnp.where(in_r0, cand[0], jnp.where(in_r1, cand[1], cand[2])))
            t0, t1 = halves
            re = jnp.where(low, t0, swap_halves(t1))
            im = jnp.where(low, swap_halves(t0), t1)
            picked[qt, j, 8 * k : 8 * k + 8, :] = re
            picked[qt, j, 32 + 8 * k : 40 + 8 * k, :] = im
        pieces[qt, j] = picked[qt, j].astype(BF16)
        return carry

    picked = esend
    lax.fori_loop(0, 8, pick, 0)

    def piece_copy(dq, dj):
        return pltpu.make_async_remote_copy(
            src_ref=pieces.at[mate_class(dq), core_of(dj)], dst_ref=win.at[cut, q],
            send_sem=b_send.at[2 * dq + dj], recv_sem=b_recv.at[2 * dq + dj],
            device_id={"cuts": cut_of(dj), "scan": mate(dq)}, device_id_type=MESH,
        )

    for dj in range(2):
        for dq in range(4):
            if dj or dq:
                piece_copy(dq, dj).start()
    win[cut, q] = pieces[q, core]
    for dj in range(2):
        for dq in range(4):
            if dj or dq:
                piece_copy(dq, dj).wait()

    def win_copy(d, k):
        return pltpu.make_async_remote_copy(
            src_ref=win.at[2 * x + k], dst_ref=win.at[2 * x + k],
            send_sem=c_send.at[2 * (d - 1) + k], recv_sem=c_recv.at[2 * (d - 1) + k],
            device_id={"cuts": 2 * lax.rem(x + d, 4) + core, "scan": me}, device_id_type=MESH,
        )

    def win_arrival(s, src_x, k):
        d = lax.rem(x - src_x + 4, 4)
        return pltpu.make_async_remote_copy(
            src_ref=win.at[s], dst_ref=win.at[s],
            send_sem=c_send.at[2 * (d - 1) + k], recv_sem=c_recv.at[2 * (d - 1) + k],
            device_id={"cuts": 2 * src_x + core, "scan": me}, device_id_type=MESH,
        )

    for k in range(2):
        for d in (1, 3, 2):
            win_copy(d, k).start()

    def window(s):
        re = jnp.concatenate([win[s, i, 0:32, :] for i in range(4)], 0)
        im = jnp.concatenate([win[s, i, 32:64, :] for i in range(4)], 0)
        return jnp.concatenate([re, im], 1).astype(F32)

    def pair(i):
        return (tab_ref[i, 0], tab_ref[i, 1])

    def forward(s, carry):
        @pl.when(s // 2 != x)
        def _():
            win_arrival(s, s // 2, s % 2).wait_recv()

        psi = wave[...]
        psis[s] = psi
        wave[...] = complex_mul(psi, window(s))

        @pl.when(s < 7)
        def _():
            wave[...] = sandwich(wave[...], pair(0), pair(1))

        return carry

    lax.fori_loop(0, 8, forward, 0)

    far = sandwich(wave[...], pair(2), pair(3))
    far_re, far_im = far[:, :WIN], far[:, WIN:]
    live = aux_ref[pl.ds(4 + core, 1), :]
    excess = (far_re * far_re + far_im * far_im - inten_ref[core]) * live
    wave[...] = sandwich(jnp.concatenate([excess * far_re, -(excess * far_im)], 1), pair(2), pair(4))

    def grad_copy(k, dq, dj):
        return pltpu.make_async_remote_copy(
            src_ref=esend.at[mate_class(dq), k], dst_ref=erecv.at[q, core],
            send_sem=e_send.at[2 * dq + dj], recv_sem=e_recv.at[2 * dq + dj],
            device_id={"cuts": cut_of(dj), "scan": mate(dq)}, device_id_type=MESH,
        )

    def backward(n, carry):
        s = 7 - n
        u = wave[...]

        @pl.when(s // 2 == x)
        def _():
            g = complex_mul(psis[s], u)
            for i in range(4):
                esend[i, s % 2, 0:32, :] = g[32 * i : 32 * i + 32, :WIN]
                esend[i, s % 2, 32:64, :] = -g[32 * i : 32 * i + 32, WIN:]

            @pl.when(s % 2 == core)
            def _():
                for dq in range(1, 4):
                    grad_copy(s % 2, dq, 0).start()

            @pl.when(s % 2 != core)
            def _():
                for dq in range(4):
                    grad_copy(s % 2, dq, 1).start()

        @pl.when(s > 2 * x)
        def _():
            wave[...] = sandwich(complex_mul(u, window(s)), pair(0), pair(1))

        return carry

    lax.fori_loop(0, 8 - 2 * x, backward, 0)
    erecv[q, core] = esend[q, core]
    for dj in range(2):
        for dq in range(4):
            if dj or dq:
                grad_copy(core_of(dj), dq, dj).wait()

    def place(k, carry):
        sums = [[[jnp.zeros(tile, F32) for _ in range(3)] for _ in range(3)] for _ in range(2)]
        for qs in range(4):
            for j in range(2):
                a = aux_all[qs, 2 * j : 2 * j + 1, :].astype(jnp.int32)
                b = aux_all[qs, 2 * j + 1 : 2 * j + 2, :].astype(jnp.int32)
                row = (sub & 3) + 8 * (sub >> 2) + (16 * bit_b + 4 * bit_a + 32 * k) - a
                in_c = [((lane + WIN * c - b) & -WIN) == 0 for c in range(3)]
                for plane in range(2):
                    val = erecv[qs, j, pl.ds(pl.multiple_of(32 * plane + 8 * k, 8), 8), :]
                    for third in range(3):
                        kept = jnp.where(((row + WIN * third) & -WIN) == 0, val, 0.0)
                        for c in range(3):
                            sums[plane][third][c] += jnp.where(in_c[c], kept, 0.0)
        for third in range(3):
            for c in range(3):
                re, im = sums[0][third][c], sums[1][third][c]
                fsend[third * 8 + 2 * k, 8 * c : 8 * c + 8, :] = jnp.where(low, re, swap_halves(im))
                fsend[third * 8 + 2 * k + 1, 8 * c : 8 * c + 8, :] = jnp.where(low, swap_halves(re), im)
        return carry

    lax.fori_loop(0, 4, place, 0)

    def sum_copy(d):
        to = lax.rem(my_slot + d, 24)
        return pltpu.make_async_remote_copy(
            src_ref=fsend.at[to], dst_ref=frecv.at[my_slot], send_sem=f_send.at[d], recv_sem=f_recv.at[d],
            device_id={"cuts": cut, "scan": owner(to)}, device_id_type=MESH,
        )

    def start_sums(d, carry):
        sum_copy(d).start()
        return carry

    lax.fori_loop(1, 24, start_sums, 0)
    frecv[my_slot] = fsend[my_slot]

    for k in range(2):
        for d in (1, 3, 2):
            win_copy(d, k).wait_send()

    def wait_sums(d, carry):
        sum_copy(d).wait()
        return carry

    lax.fori_loop(1, 24, wait_sums, 0)
    total = frecv[0]
    for i in range(1, 24):
        total = total + frecv[i]
    out_ref[...] = total * GRAD_SCALE


def body(tab, object_slices, probe_wave, intensity, positions, counts):
    slots = jnp.arange(2, dtype=jnp.int32)
    live = (slots < counts[0]).astype(F32)
    rows = jnp.concatenate([positions.astype(F32).reshape(4), live, jnp.zeros((2,), F32)])
    aux = jnp.broadcast_to(rows[:, None], (8, WIN))
    obj = object_slices.reshape(2, 4, 3, WIN).transpose(2, 0, 1, 3).reshape(24, WIN)
    vmem = pl.BlockSpec(memory_space=pltpu.VMEM)
    dma = pltpu.SemaphoreType.DMA
    out = pl.pallas_call(
        kernel,
        out_shape=jax.ShapeDtypeStruct((24, WIN), F32),
        in_specs=[vmem] * 5,
        out_specs=vmem,
        scratch_shapes=[
            pltpu.VMEM((24, 24, WIN), BF16),
            pltpu.VMEM((24, 24, WIN), F32),
            pltpu.VMEM((4, 8, WIN), F32),
            pltpu.VMEM((4, 2, 64, WIN), BF16),
            pltpu.VMEM((8, 4, 64, WIN), BF16),
            pltpu.VMEM((8, WIN, 2 * WIN), F32),
            pltpu.VMEM((WIN, 2 * WIN), F32),
            pltpu.VMEM((4, 2, 64, WIN), F32),
            pltpu.VMEM((4, 2, 64, WIN), F32),
            pltpu.VMEM((24, 24, WIN), F32),
            pltpu.VMEM((24, 24, WIN), F32),
            dma((24,)), dma((24,)), dma((4,)), dma((4,)), dma((8,)), dma((8,)),
            dma((6,)), dma((6,)), dma((8,)), dma((8,)), dma((24,)), dma((24,)), dma((1,)),
        ],
        compiler_params=pltpu.CompilerParams(
            collective_id=0, has_side_effects=True, vmem_limit_bytes=32 << 20
        ),
    )(obj, aux, probe_wave, intensity, tab)
    return out.reshape(3, 2, 4, WIN).transpose(1, 2, 0, 3).reshape(1, 2, 12 * WIN)


def solution(mesh):
    tab = tables()
    in_specs = (P("cuts", None, "scan"), P(), P("scan", None, None), P("scan", None), P("scan"))
    out_specs = P("cuts", None, "scan")
    return jax.shard_map(
        functools.partial(body, tab), mesh=mesh, in_specs=in_specs, out_specs=out_specs, check_vma=False
    )
```

time: 717 us -> 74.4 us (0.10)
  waiting for transfers between devices: 422 us -> 0 us
  starting transfers between devices: 142 us -> 0 us
  Pallas kernels: 0 us -> 66.9 us
  blocking collectives: 66 us -> 0 us
  local copies, waits for them, and re-layouts: 39.5 us -> 4.61 us
  between operations: 13.6 us -> 0.69 us
  matrix products: 10.7 us -> 0 us
  loops' own time: 8.68 us -> 0 us
  other arithmetic: 7.93 us -> 0.76 us
    psum x1 -> x0, waiting for transfers between devices: 224 us -> none  [body(): summed = lax.psum(flat_grad, 'scan')]
    ppermute x32 -> x0, waiting for transfers between devices: 197 us -> none  [shifted(): return lax.ppermute(x, axis, pairs)]
    ppermute x32 -> x0, starting transfers between devices: 142 us -> none  [shifted(): return lax.ppermute(x, axis, pairs)]
    pallas_call x0 -> x1, Pallas kernels: none -> 66.9 us  [body(): pl.pallas_call(kernel, out_shape=jax.ShapeDtypeStruct((24, WIN), F32), in...]
    all_gather x1 -> x0, blocking collectives: 66 us -> none  [body(): whole_slices = lax.all_gather(object_slices, 'scan', axis=2, tiled=True)]
    another operation x51 -> x1, local copies, waits for them, and re-layouts: 23.2 us -> 0.01 us
    dot_general x20 -> x0, matrix products: 10.7 us -> none  [the longest x2 3.07 us: sandwich(): contract('bij,jk->bik', mid_im, right_im)]
    another operation x22 -> x0, loops' own time: 8.68 us -> none  [the longest x1 7.42 us: add_windows(): return lax.fori_loop(0, corners.shape[0], add_one, plane)]
  transfers between devices with their start and end apart: 33 -> 0, of which waited for: 29 -> 0; matrix products, arithmetic and copies ran while one was open for 0% -> 0% of each run, Pallas kernels for 0% -> 0%
where the time goes in v1:
time: 74.4 us; the launch traced here: 73 us
  Pallas kernels  66.9 us (90%)
  local copies, waits for them, and re-layouts  4.61 us (6%)
  other arithmetic  0.76 us (1%)
    pallas_call x1, Pallas kernels, body(): pl.pallas_call(kernel, out_shape=jax.ShapeDtypeStruct((24, WIN), F32), in...  66.9 us
    unnamed x6, local copies, waits for them, and re-layouts  3.12 us

profile of v1, /device:TPU:1, one launch (start us, length us, event | category | flops | bytes accessed | tf_op | source)
XLA Modules:
  0.0 73.0 jit_solution(12401391085563214931)
XLA Ops:
  0.7 0.7 convert_element_type.6
  1.3 0.1 reshape.18
  1.4 0.1 pad_maximum_fusion
  1.5 0.1 broadcast_in_dim.2.aux_ref
  1.6 0.7 reshape.16
  2.3 0.0 copy-start
  2.3 1.3 %copy-done = bf16[5,2,256,256]{3,2,1,0:T(8,128)(2,1)S(1)} copy-done((bf16[5,2,256,256]{3,2,1,0:T(8,128)(2,1)S(1)}, bf16[5,2,256,256]{3,2,1,0:T(8,128)(2,1)}, u32[]{:S(2)}) %copy-start) | copy-done | bytes 1310744
  3.6 0.0 copy-start.1
  3.6 0.9 %copy-done.1 = f32[2,128,128]{2,1,0:T(8,128)S(1)} copy-done((f32[2,128,128]{2,1,0:T(8,128)S(1)}, f32[2,128,128]{2,1,0:T(8,128)}, u32[]{:S(2)}) %copy-start.1) | copy-done | bytes 131096
  4.5 0.0 copy-start.2
  4.5 0.9 %copy-done.2 = f32[2,128,128]{2,1,0:T(8,128)S(1)} copy-done((f32[2,128,128]{2,1,0:T(8,128)S(1)}, f32[2,128,128]{2,1,0:T(8,128)}, u32[]{:S(2)}) %copy-start.2) | copy-done | bytes 131096
  5.4 66.9 %shard_map.64 = f32[24,128]{1,0:T(8,128)S(1)} custom-call(bf16[24,128]{1,0:T(8,128)(2,1)S(1)} %bitcast.9, f32[8,128]{1,0:T(8,128)S(1)} %broadcast_in_dim.2.aux_ref, f32[2,128,128]{2,1,0:T(8,128)S(1)} %copy-done.1, f32[2,128,128]{2,1,0:T(8,128)S(1)} %copy-done.2, bf16[5,2,256,256]{3,2,1,0:T(8,128)(2,1)S(1)} %copy-done), custom_call_target="tpu_custom_call" | custom-call | tf_op jit(solution)/shard_map/pallas_call | solution.py:405
  72.4 0.6 reshape.20
  (4 shorter events, 0.0 us)
Async XLA Ops:
  2.3 1.3 %copy-start = (bf16[5,2,256,256]{3,2,1,0:T(8,128)(2,1)S(1)}, bf16[5,2,256,256]{3,2,1,0:T(8,128)(2,1)}, u32[]{:S(2)}) copy-start(bf16[5,2,256,256]{3,2,1,0:T(8,128)(2,1)} %constant.4.clone.tab_ref) | copy-start | bytes 3932164
  3.6 0.9 %copy-start.1 = (f32[2,128,128]{2,1,0:T(8,128)S(1)}, f32[2,128,128]{2,1,0:T(8,128)}, u32[]{:S(2)}) copy-start(f32[2,128,128]{2,1,0:T(8,128)} %probe_ref.1) | copy-start | bytes 393220
  4.5 0.9 %copy-start.2 = (f32[2,128,128]{2,1,0:T(8,128)S(1)}, f32[2,128,128]{2,1,0:T(8,128)}, u32[]{:S(2)}) copy-start(f32[2,128,128]{2,1,0:T(8,128)} %inten_ref.1) | copy-start | bytes 393220

commit v2 on v1

v2 whole, which is shorter than its diff:
```python
import functools

import jax
import jax.numpy as jnp
import ml_dtypes
import numpy as np
from jax import lax
from jax.experimental import pallas as pl
from jax.experimental.pallas import tpu as pltpu
from jax.sharding import PartitionSpec as P

WIN = 128
FRESNEL = 0.5
GRAD_SCALE = 0.25
NZ = 12
F32 = jnp.float32
BF16 = jnp.bfloat16
MESH = pl.DeviceIdType.MESH


def row_order():
    rho = np.arange(WIN)
    q, h, k, rr = rho // 16, (rho // 8) % 2, (rho // 4) % 2, rho % 4
    return 64 * h + 32 * k + 16 * (q // 4) + 4 * (q % 4) + rr


def split_table(mat):
    hi = mat.astype(ml_dtypes.bfloat16)
    lo = (mat - hi.astype(np.float64)).astype(ml_dtypes.bfloat16)
    return np.stack([hi, lo])


def tables():
    k = np.arange(WIN)
    four = np.exp(-2j * np.pi * ((k[:, None] * k[None, :]) % WIN) / WIN) / np.sqrt(WIN)
    freq = np.where(k < WIN // 2, k, k - WIN).astype(np.float64)
    half = np.exp(-1j * np.pi * FRESNEL * freq * freq / WIN)
    kern = np.conj(four.T) @ (half[:, None] * four)
    order = row_order()

    def right(mat):
        return split_table(np.block([[mat.real, mat.imag], [-mat.imag, mat.real]]))

    def left(mat):
        return split_table(np.block([[mat.real, -mat.imag], [mat.imag, mat.real]]))

    return np.stack(
        [
            right(kern),
            left(kern[order][:, order]),
            right(four),
            left(four[:, order]),
            left(four[order]),
        ]
    )


def dot(a, b):
    return jnp.dot(a, b, preferred_element_type=F32)


def split(x):
    hi = x.astype(BF16)
    return hi, (x - hi.astype(F32)).astype(BF16)


def sandwich(x, right, left):
    hi, lo = split(x)
    both = dot(jnp.concatenate([hi, lo], 0), right[0])
    mid = both[:WIN] + both[WIN:] + dot(hi, right[1])
    mid = jnp.concatenate([mid[:, :WIN], mid[:, WIN:]], 0)
    hi, lo = split(mid)
    both = dot(left[0], jnp.concatenate([hi, lo], 1))
    out = both[:, :WIN] + both[:, WIN:] + dot(left[1], hi)
    return jnp.concatenate([out[:WIN], out[WIN:]], 1)


def complex_mul(x, w):
    x_re, x_im, w_re, w_im = x[:, :WIN], x[:, WIN:], w[:, :WIN], w[:, WIN:]
    return jnp.concatenate([x_re * w_re - x_im * w_im, x_re * w_im + x_im * w_re], 1)


def rolled_probe(probe_ref, row_at, col_at):
    shape = (WIN, WIN)
    rho = lax.broadcasted_iota(jnp.int32, shape, 0)
    lane = lax.broadcasted_iota(jnp.int32, shape, 1)
    t = (
        64 * ((rho >> 3) & 1)
        + 32 * ((rho >> 2) & 1)
        + 16 * ((rho >> 6) & 1)
        + 4 * ((rho >> 4) & 3)
        + (rho & 3)
    )
    rows = (((t - lane - row_at) & (WIN - 1)) == 0).astype(F32).astype(BF16)
    cols = (((lane - rho - col_at) & (WIN - 1)) == 0).astype(F32).astype(BF16)
    halves = []
    for plane in range(2):
        rest = probe_ref[plane]
        total = jnp.zeros(shape, F32)
        for _ in range(3):
            part = rest.astype(BF16)
            rest = rest - part.astype(F32)
            total = total + dot(dot(rows, part).astype(BF16), cols)
        halves.append(total)
    return jnp.concatenate(halves, 1)


def swap_halves(x):
    return jnp.concatenate([x[..., 4:8, :], x[..., 0:4, :]], -2)


def rem(a, b):
    return lax.rem(a, jnp.int32(b))


def div(a, b):
    return lax.div(a, jnp.int32(b))


def kernel(
    obj_ref, pos_ref, counts_ref, probe_ref, inten_ref, tab_ref,
    out_ref,
    obj, pos, counts, probe, inten, tab,
    cells, strips, aux_all, pieces, win, psis, wave, esend, erecv, fsend, frecv,
    in_sems, near_sems, a_sem, p_sem, b_send, b_recv, e_send, e_recv, f_sem,
):
    cut = lax.axis_index("cuts")
    me = lax.axis_index("scan")
    x, core = div(cut, 2), rem(cut, 2)
    y, z = div(me, NZ), rem(me, NZ)
    z_block, z_in = div(z, 4), rem(z, 4)
    y_block, y_in = div(y, 2), rem(y, 2)
    bit_b = rem(y_in + z_block, 2)
    q = 4 * bit_b + z_in
    n_mine = div(me, 8)
    row_base = 16 * bit_b + 4 * z_in

    def far(d):
        n = rem(n_mine + d, 12)
        return n, 8 * n + 4 * bit_b + z_in

    def mate(dy, dz):
        yi, zi = rem(y_in + dy, 2), rem(z_in + dz, 4)
        return 4 * yi + zi, 4 * rem(yi + z_block, 2) + zi, (2 * y_block + yi) * NZ + 4 * z_block + zi

    def at(cut_to, scan_to):
        return dict(device_id={"cuts": cut_to, "scan": scan_to}, device_id_type=MESH)

    sibling = cut + 1 - 2 * core

    def chip_at(i):
        x_to = i + (x <= i).astype(jnp.int32)
        return 2 * x_to + core

    loads = [
        (obj_ref, obj), (pos_ref, pos), (counts_ref, counts), (probe_ref, probe), (inten_ref.at[core], inten), (tab_ref, tab),
    ]
    loads = [pltpu.make_async_copy(src, dst, in_sems.at[i]) for i, (src, dst) in enumerate(loads)]
    for load in loads:
        load.start()

    barrier = pltpu.get_barrier_semaphore()
    for d in range(1, 12):
        pl.semaphore_signal(barrier, inc=1, **at(cut, far(d)[1]))
    for d in range(1, 4):
        pl.semaphore_signal(barrier, inc=1, **at(cut, mate(0, d)[2]))
    pl.semaphore_signal(barrier, inc=1, **at(cut, mate(1, 0)[2]))
    pl.semaphore_signal(barrier, inc=1, **at(sibling, me))
    for i in range(3):
        pl.semaphore_signal(barrier, inc=1, **at(chip_at(i), me))
    loads[0].wait()
    pl.semaphore_wait(barrier, 19)

    for d in range(1, 12):
        pltpu.make_async_remote_copy(
            src_ref=obj, dst_ref=cells.at[n_mine], send_sem=a_sem.at[0], recv_sem=a_sem.at[1], **at(cut, far(d)[1])
        ).start()
    cells[n_mine] = obj[...]

    pl.semaphore_signal(near_sems.at[0], inc=1, **at(cut, mate(1, 0)[2]))
    loads[1].wait()
    loads[2].wait()
    here = 4 * y_in + z_in
    sub = lax.broadcasted_iota(jnp.int32, (8, WIN), 0)
    lane = lax.broadcasted_iota(jnp.int32, (8, WIN), 1)
    mine = jnp.where(
        sub == 0, pos[0, 0], jnp.where(sub == 1, pos[0, 1], jnp.where(sub == 2, pos[1, 0], pos[1, 1]))
    )
    aux_all[here] = mine
    pl.semaphore_wait(near_sems.at[0], 1)
    pl.semaphore_signal(near_sems.at[1], inc=1, **at(sibling, me))
    for d in range(1, 8):
        pltpu.make_async_remote_copy(
            src_ref=aux_all.at[here], dst_ref=aux_all.at[here],
            send_sem=p_sem.at[0], recv_sem=p_sem.at[1], **at(cut, mate(d // 4, d % 4)[2])
        ).start()
    pl.semaphore_wait(near_sems.at[1], 1)
    for i in range(3):
        pl.semaphore_signal(near_sems.at[2], inc=1, **at(chip_at(i), me))

    loads[3].wait()
    row_at = jnp.where(core == 0, pos[0, 0], pos[1, 0])
    col_at = jnp.where(core == 0, pos[0, 1], pos[1, 1])
    wave[...] = rolled_probe(probe, row_at, col_at)
    loads[5].wait()

    pltpu.make_async_copy(aux_all.at[0:7], aux_all.at[0:7], p_sem.at[1]).wait()
    pl.semaphore_wait(near_sems.at[2], 3)
    pltpu.make_async_copy(cells.at[0:11], cells.at[0:11], a_sem.at[1]).wait()

    blocks = [cells[n].astype(F32) for n in range(12)]
    for third in range(3):
        for h in range(2):
            for c in range(3):
                for plane in range(2):
                    first = 8 * c + 4 * plane
                    rows = [blocks[4 * third + 2 * h + k][first : first + 4] for k in range(2)]
                    strips[third, h, c, plane] = jnp.concatenate(rows, 0)

    low = sub < 4
    row_here = 32 * (sub >> 2) + (sub & 3) + row_base

    def masks(p, j):
        a = aux_all[p, 2 * j : 2 * j + 1, :]
        b = aux_all[p, 2 * j + 1 : 2 * j + 2, :]
        in_row = [[((row_here + (WIN * third + 64 * h) - a) & -WIN) == 0 for third in range(3)] for h in range(2)]
        in_col = [((lane + WIN * c - b) & -WIN) == 0 for c in range(3)]
        return in_row, in_col

    def pick(p):
        for j in range(2):
            in_row, in_col = masks(p, j)
            tiles = []
            for plane in range(2):
                for h in range(2):
                    cand = []
                    for third in range(3):
                        c0, c1, c2 = (strips[third, h, c, plane] for c in range(3))
                        cand.append(jnp.where(in_col[0], c0, jnp.where(in_col[1], c1, c2)))
                    tiles.append(jnp.where(in_row[h][0], cand[0], jnp.where(in_row[h][1], cand[1], cand[2])))
            pieces[2 * p + j] = jnp.concatenate(tiles, 0).astype(BF16)

    def piece_send(p, j, x_to, to):
        pltpu.make_async_remote_copy(
            src_ref=pieces.at[2 * p + j], dst_ref=win.at[cut, q],
            send_sem=b_send, recv_sem=b_recv.at[cut], **at(2 * x_to + j, to)
        ).start()

    def own_pieces(x_to):
        piece_send(here, 1 - core, x_to, me)

        @pl.when(x != x_to)
        def _():
            piece_send(here, core, x_to, me)

    pick(here)
    pltpu.make_async_copy(pieces.at[2 * here + core], win.at[cut, q], b_recv.at[cut]).start()
    own_pieces(0)

    def pick_and_send(d, carry):
        p, _, to = mate(div(d, 4), rem(d, 4))
        pick(p)
        for j in range(2):
            piece_send(p, j, 0, to)
        return carry

    lax.fori_loop(1, 8, pick_and_send, 0)
    for x_to in range(1, 4):
        own_pieces(x_to)

        def only_send(d, carry):
            p, _, to = mate(div(d, 4), rem(d, 4))
            for j in range(2):
                piece_send(p, j, x_to, to)
            return carry

        lax.fori_loop(1, 8, only_send, 0)

    def window(s):
        w = win[s].astype(F32)
        return jnp.concatenate([w[:, 0:16].reshape(WIN, WIN), w[:, 16:32].reshape(WIN, WIN)], 1)

    def pair(i):
        return (tab[i, 0], tab[i, 1])

    def forward(s, carry):
        pltpu.make_async_copy(win.at[s], win.at[s], b_recv.at[s]).wait()
        psi = wave[...]
        psis[s] = psi
        wave[...] = complex_mul(psi, window(s))

        @pl.when(s < 7)
        def _():
            wave[...] = sandwich(wave[...], pair(0), pair(1))

        return carry

    lax.fori_loop(0, 8, forward, 0)
    loads[4].wait()

    far_field = sandwich(wave[...], pair(2), pair(3))
    far_re, far_im = far_field[:, :WIN], far_field[:, WIN:]
    live = jnp.where(core < counts[0], 1.0, 0.0).astype(F32)
    excess = (far_re * far_re + far_im * far_im - inten[...]) * live
    wave[...] = sandwich(jnp.concatenate([excess * far_re, -(excess * far_im)], 1), pair(2), pair(4))

    def backward(n, carry):
        s = 7 - n
        u = wave[...]

        @pl.when(div(s, 2) == x)
        def _():
            k = rem(s, 2)
            g = complex_mul(psis[s], u)
            esend[k] = jnp.concatenate(
                [g[:, :WIN].reshape(8, 16, WIN), -g[:, WIN:].reshape(8, 16, WIN)], 1
            )

            def send(d, carry):
                _, q_to, to = mate(div(d, 4), rem(d, 4))
                pltpu.make_async_remote_copy(
                    src_ref=esend.at[k, q_to], dst_ref=erecv.at[core, here],
                    send_sem=e_send, recv_sem=e_recv.at[core], **at(s, to)
                ).start()
                return carry

            @pl.when(k != core)
            def _():
                send(0, 0)

            @pl.when(k == core)
            def _():
                pltpu.make_async_copy(esend.at[k, q], erecv.at[core, here], e_recv.at[core]).start()

            lax.fori_loop(1, 8, send, 0)

        @pl.when(s > 2 * x)
        def _():
            wave[...] = sandwich(complex_mul(u, window(s)), pair(0), pair(1))

        return carry

    lax.fori_loop(0, 8 - 2 * x, backward, 0)

    for j in range(2):
        pltpu.make_async_copy(erecv.at[j], erecv.at[j], e_recv.at[j]).wait()

    def place(p, sums):
        sums = list(sums)
        for j in range(2):
            in_row, in_col = masks(p, j)
            for plane in range(2):
                for h in range(2):
                    val = erecv[j, p, 16 * plane + 8 * h : 16 * plane + 8 * h + 8, :]
                    for third in range(3):
                        kept = jnp.where(in_row[h][third], val, 0.0)
                        for c in range(3):
                            i = ((third * 2 + h) * 3 + c) * 2 + plane
                            sums[i] = sums[i] + jnp.where(in_col[c], kept, 0.0)
        return tuple(sums)

    sums = lax.fori_loop(0, 8, place, tuple(jnp.zeros((8, WIN), F32) for _ in range(36)))
    for half in range(6):
        for c in range(3):
            re, im = sums[(half * 3 + c) * 2], sums[(half * 3 + c) * 2 + 1]
            fsend[2 * half, 8 * c : 8 * c + 8, :] = jnp.where(low, re, swap_halves(im))
            fsend[2 * half + 1, 8 * c : 8 * c + 8, :] = jnp.where(low, swap_halves(re), im)

    for d in range(1, 12):
        n_to, to = far(d)
        pltpu.make_async_remote_copy(
            src_ref=fsend.at[n_to], dst_ref=frecv.at[n_mine], send_sem=f_sem.at[0], recv_sem=f_sem.at[1], **at(cut, to)
        ).start()
    frecv[n_mine] = fsend[n_mine]

    flat = win.reshape(64, 32, WIN)
    flat_e = esend.reshape(16, 32, WIN)
    for ref, sem in (
        (cells.at[0:11], a_sem.at[0]),
        (aux_all.at[0:7], p_sem.at[0]),
        (flat.at[0:63], b_send),
        (flat_e.at[0:15], e_send),
        (fsend.at[0:11], f_sem.at[0]),
        (frecv.at[0:11], f_sem.at[1]),
    ):
        pltpu.make_async_copy(ref, ref, sem).wait()
    total = frecv[0]
    for n in range(1, 12):
        total = total + frecv[n]
    out_ref[...] = total * GRAD_SCALE


def body(tab, object_slices, probe_wave, intensity, positions, counts):
    obj = object_slices.reshape(2, 4, 3, WIN).transpose(2, 0, 1, 3).reshape(24, WIN)
    hbm = pl.BlockSpec(memory_space=pltpu.HBM)
    vmem = pl.BlockSpec(memory_space=pltpu.VMEM)
    dma = pltpu.SemaphoreType.DMA
    out = pl.pallas_call(
        kernel,
        out_shape=jax.ShapeDtypeStruct((24, WIN), F32),
        in_specs=[hbm] * 6,
        out_specs=vmem,
        scratch_shapes=[
            pltpu.VMEM((24, WIN), BF16),
            pltpu.SMEM((2, 2), jnp.int32),
            pltpu.SMEM((1,), jnp.int32),
            pltpu.VMEM((2, WIN, WIN), F32),
            pltpu.VMEM((WIN, WIN), F32),
            pltpu.VMEM((5, 2, 2 * WIN, 2 * WIN), BF16),
            pltpu.VMEM((12, 24, WIN), BF16),
            pltpu.VMEM((3, 2, 3, 2, 8, WIN), F32),
            pltpu.VMEM((8, 8, WIN), jnp.int32),
            pltpu.VMEM((16, 32, WIN), BF16),
            pltpu.VMEM((8, 8, 32, WIN), BF16),
            pltpu.VMEM((8, WIN, 2 * WIN), F32),
            pltpu.VMEM((WIN, 2 * WIN), F32),
            pltpu.VMEM((2, 8, 32, WIN), F32),
            pltpu.VMEM((2, 8, 32, WIN), F32),
            pltpu.VMEM((12, 24, WIN), F32),
            pltpu.VMEM((12, 24, WIN), F32),
            dma((6,)),
            pltpu.SemaphoreType.REGULAR((3,)),
            dma((2,)), dma((2,)),
            dma, dma((8,)),
            dma, dma((2,)),
            dma((2,)),
        ],
        compiler_params=pltpu.CompilerParams(
            collective_id=0, has_side_effects=True, vmem_limit_bytes=63 << 20
        ),
    )(obj, positions, counts, probe_wave, intensity, tab)
    return out.reshape(3, 2, 4, WIN).transpose(1, 2, 0, 3).reshape(1, 2, 12 * WIN)


def solution(mesh):
    tab = tables()
    in_specs = (P("cuts", None, "scan"), P(), P("scan", None, None), P("scan", None), P("scan"))
    out_specs = P("cuts", None, "scan")
    return jax.shard_map(
        functools.partial(body, tab), mesh=mesh, in_specs=in_specs, out_specs=out_specs, check_vma=False
    )
```

time: 74.4 us -> 65.4 us (0.88)
  the two profiles are of different devices: /device:TPU:1 before, /device:TPU:2 now
where the time goes in v2:
time: 65.4 us; the launch traced here: 65.1 us
  Pallas kernels  61.8 us (94%)
  local copies, waits for them, and re-layouts  2.64 us (4%)
  between operations  0.66 us (1%)
    pallas_call x1, Pallas kernels, body(): pl.pallas_call(kernel, out_shape=jax.ShapeDtypeStruct((24, WIN), F32), in...  61.8 us
    reshape x2, local copies, waits for them, and re-layouts, body(): out.reshape(3, 2, 4, WIN).transpose(1, 2, 0, 3).reshape(1, 2, 12 * WIN)  1.33 us

profile of v2, /device:TPU:2, one launch (start us, length us, event | category | flops | bytes accessed | tf_op | source)
XLA Modules:
  0.0 65.1 jit_solution(16670263428258264517)
XLA Ops:
  0.7 0.7 %reshape.12 = bf16[2,4,3,128]{3,2,1,0:T(4,128)(2,1)S(1)} reshape(bf16[1,2,1536]{2,1,0:T(2,128)(2,1)} %param.6) | data formatting | bytes 12288 | tf_op jit(solution)/shard_map/reshape | solution.py:394
  1.4 0.6 copy.9
  2.0 61.8 %shard_map.64 = f32[24,128]{1,0:T(8,128)} custom-call(bf16[24,128]{1,0:T(8,128)(2,1)} %bitcast.9, s32[2,2]{1,0:T(2,128)} %pos_ref.1, s32[1]{0:T(128)S(6)} %copy.13.counts_ref, f32[2,128,128]{2,1,0:T(8,128)} %probe_ref.1, f32[2,128,128]{2,1,0:T(8,128)} %inten_ref.1, bf16[5,2,256,256]{3,2,1,0:T(8,128)(2,1)} %constant.2.clone.tab_ref), custom_call_target="tpu_custom_call" | custom-call | tf_op jit(solution)/shard_map/pallas_call | solution.py:398
  63.8 0.7 %copy.12 = f32[3,2,4,128]{3,0,2,1:T(4,128)S(1)} copy(f32[3,2,4,128]{3,2,1,0:T(4,128)} %bitcast.7) | data formatting | bytes 24576 | tf_op jit(solution)/shard_map/reshape | solution.py:432
  64.5 0.6 reshape.15

commit v3 on v2

v3 whole, which is shorter than its diff:
```python
import functools

import jax
import jax.numpy as jnp
import ml_dtypes
import numpy as np
from jax import lax
from jax.experimental import pallas as pl
from jax.experimental.pallas import tpu as pltpu
from jax.sharding import PartitionSpec as P

WIN = 128
FRESNEL = 0.5
GRAD_SCALE = 0.25
NZ = 12
F32 = jnp.float32
BF16 = jnp.bfloat16
MESH = pl.DeviceIdType.MESH


def row_order():
    rho = np.arange(WIN)
    q, k, rr = rho // 8, (rho // 4) % 2, rho % 4
    return 64 * k + 16 * (q // 4) + 4 * (q % 4) + rr


def split_table(mat):
    hi = mat.astype(ml_dtypes.bfloat16)
    lo = (mat - hi.astype(np.float64)).astype(ml_dtypes.bfloat16)
    return np.stack([hi, lo])


def tables():
    k = np.arange(WIN)
    four = np.exp(-2j * np.pi * ((k[:, None] * k[None, :]) % WIN) / WIN) / np.sqrt(WIN)
    freq = np.where(k < WIN // 2, k, k - WIN).astype(np.float64)
    half = np.exp(-1j * np.pi * FRESNEL * freq * freq / WIN)
    kern = np.conj(four.T) @ (half[:, None] * four)
    order = row_order()

    def right(mat):
        return split_table(np.block([[mat.real, mat.imag], [-mat.imag, mat.real]]))

    def left(mat):
        return split_table(np.block([[mat.real, -mat.imag], [mat.imag, mat.real]]))

    return np.stack(
        [
            right(kern),
            left(kern[order][:, order]),
            right(four),
            left(four[:, order]),
            left(four[order]),
        ]
    )


def dot(a, b):
    return jnp.dot(a, b, preferred_element_type=F32)


def split(x):
    hi = x.astype(BF16)
    return hi, (x - hi.astype(F32)).astype(BF16)


def sandwich(x, right, left):
    hi, lo = split(x)
    both = dot(jnp.concatenate([hi, lo], 0), right[0])
    mid = both[:WIN] + both[WIN:] + dot(hi, right[1])
    mid = jnp.concatenate([mid[:, :WIN], mid[:, WIN:]], 0)
    hi, lo = split(mid)
    both = dot(left[0], jnp.concatenate([hi, lo], 1))
    out = both[:, :WIN] + both[:, WIN:] + dot(left[1], hi)
    return jnp.concatenate([out[:WIN], out[WIN:]], 1)


def complex_mul(x, w):
    x_re, x_im, w_re, w_im = x[:, :WIN], x[:, WIN:], w[:, :WIN], w[:, WIN:]
    return jnp.concatenate([x_re * w_re - x_im * w_im, x_re * w_im + x_im * w_re], 1)


def rolled_probe(probe_ref, row_at, col_at):
    shape = (WIN, WIN)
    rho = lax.broadcasted_iota(jnp.int32, shape, 0)
    lane = lax.broadcasted_iota(jnp.int32, shape, 1)
    t = 64 * ((rho >> 2) & 1) + 16 * ((rho >> 5) & 3) + 4 * ((rho >> 3) & 3) + (rho & 3)
    rows = (((t - lane - row_at) & (WIN - 1)) == 0).astype(F32).astype(BF16)
    cols = (((lane - rho - col_at) & (WIN - 1)) == 0).astype(F32).astype(BF16)
    halves = []
    for plane in range(2):
        rest = probe_ref[plane]
        total = jnp.zeros(shape, F32)
        for _ in range(3):
            part = rest.astype(BF16)
            rest = rest - part.astype(F32)
            total = total + dot(dot(rows, part).astype(BF16), cols)
        halves.append(total)
    return jnp.concatenate(halves, 1)


def swap_halves(x):
    return jnp.concatenate([x[..., 4:8, :], x[..., 0:4, :]], -2)


STEPS = 256
TOP = 32760.0


def scale_of(steps):
    return jnp.exp(steps.astype(F32) * (np.log(2.0) / STEPS))


def pack(re, im):
    most = jnp.maximum(jnp.abs(re), jnp.abs(im)).reshape(4, 4, 8, WIN)
    most = jnp.max(jnp.max(most, axis=1), axis=1, keepdims=True)
    steps = jnp.ceil(jnp.log(jnp.maximum(most, 1e-30)) * (STEPS / np.log(2.0))).astype(jnp.int32)
    factor = (TOP * scale_of(-steps))[:, None]
    whole_re, whole_im = (
        jnp.floor(part.reshape(4, 4, 8, WIN) * factor + 0.5).astype(jnp.int32) for part in (re, im)
    )
    both = ((whole_re << 16) | (whole_im & 0xFFFF)).reshape(16, 8, WIN)
    steps = jnp.broadcast_to(steps[:, None], (4, 4, 1, WIN)).reshape(16, 1, WIN)
    return jnp.concatenate([both, steps], 1)


def rem(a, b):
    return lax.rem(a, jnp.int32(b))


def div(a, b):
    return lax.div(a, jnp.int32(b))


def kernel(
    obj_ref, pos_ref, counts_ref, probe_ref, inten_ref, tab_ref,
    out_ref,
    raw, obj, pos, counts, probe, inten, tab,
    cells, strips, aux_all, pieces, win, psis, wave, esend, erecv, fsend, frecv,
    in_sems, near_sems, a_sem, p_sem, b_send, b_recv, e_send, e_recv, f_sem,
):
    cut = lax.axis_index("cuts")
    me = lax.axis_index("scan")
    x, core = div(cut, 2), rem(cut, 2)
    y, z = div(me, NZ), rem(me, NZ)
    z_block, z_in = div(z, 4), rem(z, 4)
    y_block, y_in = div(y, 4), rem(y, 4)
    bit_b = rem(3 * y_in + z_block, 4)
    q = 4 * bit_b + z_in
    n_mine = div(me, 16)
    row_base = 16 * bit_b + 4 * z_in

    def worker(yi, zi, j):
        return rem(yi + zi + 2 * j, 4)

    working = x == worker(y_in, z_in, core)

    def far(d):
        n = rem(n_mine + d, 6)
        return n, 16 * n + 4 * bit_b + z_in

    def mate(dy, dz):
        yi, zi = rem(y_in + dy, 4), rem(z_in + dz, 4)
        return yi, zi, 4 * rem(3 * yi + z_block, 4) + zi, (4 * y_block + yi) * NZ + 4 * z_block + zi

    def at(cut_to, scan_to):
        return dict(device_id={"cuts": cut_to, "scan": scan_to}, device_id_type=MESH)

    sibling = cut + 1 - 2 * core

    def chip_at(i):
        x_to = i + (x <= i).astype(jnp.int32)
        return 2 * x_to + core

    loads = [
        (obj_ref.at[0], raw), (pos_ref, pos), (counts_ref, counts), (probe_ref, probe), (inten_ref.at[core], inten), (tab_ref, tab),
    ]
    loads = [pltpu.make_async_copy(src, dst, in_sems.at[i]) for i, (src, dst) in enumerate(loads)]
    for load in loads:
        load.start()

    barrier = pltpu.get_barrier_semaphore()
    for d in range(1, 6):
        pl.semaphore_signal(barrier, inc=1, **at(cut, far(d)[1]))
    for d in range(1, 4):
        pl.semaphore_signal(barrier, inc=1, **at(cut, mate(0, d)[3]))
        pl.semaphore_signal(barrier, inc=1, **at(cut, mate(d, 0)[3]))
    pl.semaphore_signal(barrier, inc=1, **at(sibling, me))
    for i in range(3):
        pl.semaphore_signal(barrier, inc=1, **at(chip_at(i), me))

    loads[0].wait()
    flat_obj = raw[...].astype(F32)
    rows = []
    for c in range(3):
        for plane in range(2):
            for rr in range(4):
                first = (3 * rr + c) * WIN
                rows.append(flat_obj[plane : plane + 1, first : first + WIN])
    obj[...] = jnp.concatenate(rows, 0).astype(BF16)
    pl.semaphore_wait(barrier, 15)

    for d in range(1, 4):
        pl.semaphore_signal(near_sems.at[0], inc=1, **at(cut, mate(d, 0)[3]))

    for d in range(1, 6):
        pltpu.make_async_remote_copy(
            src_ref=obj, dst_ref=cells.at[n_mine], send_sem=a_sem.at[0], recv_sem=a_sem.at[1], **at(cut, far(d)[1])
        ).start()
    cells[n_mine] = obj[...]

    loads[1].wait()
    loads[2].wait()
    here = 4 * y_in + z_in
    sub = lax.broadcasted_iota(jnp.int32, (8, WIN), 0)
    lane = lax.broadcasted_iota(jnp.int32, (8, WIN), 1)
    mine = jnp.where(
        sub == 0, pos[0, 0], jnp.where(sub == 1, pos[0, 1], jnp.where(sub == 2, pos[1, 0], pos[1, 1]))
    )
    aux_all[here] = mine[0:4]
    pl.semaphore_wait(near_sems.at[0], 3)
    pl.semaphore_signal(near_sems.at[1], inc=1, **at(sibling, me))
    for d in range(1, 16):
        pltpu.make_async_remote_copy(
            src_ref=aux_all.at[here], dst_ref=aux_all.at[here],
            send_sem=p_sem.at[0], recv_sem=p_sem.at[1], **at(cut, mate(d // 4, d % 4)[3])
        ).start()
    pl.semaphore_wait(near_sems.at[1], 1)
    for i in range(3):
        pl.semaphore_signal(near_sems.at[2], inc=1, **at(chip_at(i), me))

    loads[3].wait()
    loads[4].wait()
    loads[5].wait()

    @pl.when(working)
    def _():
        row_at = jnp.where(core == 0, pos[0, 0], pos[1, 0])
        col_at = jnp.where(core == 0, pos[0, 1], pos[1, 1])
        wave[...] = rolled_probe(probe, row_at, col_at)

    pltpu.make_async_copy(aux_all.at[0:15], aux_all.at[0:15], p_sem.at[1]).wait()
    pl.semaphore_wait(near_sems.at[2], 3)
    pltpu.make_async_copy(cells.at[0:5], cells.at[0:5], a_sem.at[1]).wait()

    blocks = [cells[n].astype(F32) for n in range(6)]
    for third in range(3):
        for c in range(3):
            for plane in range(2):
                first = 8 * c + 4 * plane
                rows = [blocks[2 * third + k][first : first + 4] for k in range(2)]
                strips[third, c, plane] = jnp.concatenate(rows, 0)

    low = sub < 4
    row_here = 64 * (sub >> 2) + (sub & 3) + row_base

    def masks(p, j):
        a = aux_all[p, 2 * j : 2 * j + 1, :]
        b = aux_all[p, 2 * j + 1 : 2 * j + 2, :]
        in_row = [((row_here + WIN * third - a) & -WIN) == 0 for third in range(3)]
        in_col = [((lane + WIN * c - b) & -WIN) == 0 for c in range(3)]
        return in_row, in_col

    def pick(p):
        for j in range(2):
            in_row, in_col = masks(p, j)
            planes = []
            for plane in range(2):
                cand = []
                for third in range(3):
                    c0, c1, c2 = (strips[third, c, plane] for c in range(3))
                    cand.append(jnp.where(in_col[0], c0, jnp.where(in_col[1], c1, c2)))
                planes.append(jnp.where(in_row[0], cand[0], jnp.where(in_row[1], cand[1], cand[2])))
            pieces[2 * p + j] = jnp.concatenate(planes, 0).astype(BF16)

    def piece_send(yi, zi, j, to):
        pltpu.make_async_remote_copy(
            src_ref=pieces.at[2 * (4 * yi + zi) + j], dst_ref=win.at[cut, q],
            send_sem=b_send, recv_sem=b_recv.at[cut], **at(2 * worker(yi, zi, j) + j, to)
        ).start()

    def pick_and_send(d, carry):
        yi, zi, _, to = mate(div(d, 4), rem(d, 4))
        pick(4 * yi + zi)
        for j in range(2):
            piece_send(yi, zi, j, to)
        return carry

    lax.fori_loop(1, 16, pick_and_send, 0)
    pick(here)
    piece_send(y_in, z_in, 1 - core, me)

    @pl.when(working)
    def _():
        pltpu.make_async_copy(pieces.at[2 * here + core], win.at[cut, q], b_recv.at[cut]).start()

    @pl.when(jnp.logical_not(working))
    def _():
        piece_send(y_in, z_in, core, me)

    def window(s):
        w = win[s].astype(F32)
        return jnp.concatenate([w[:, 0:8].reshape(WIN, WIN), w[:, 8:16].reshape(WIN, WIN)], 1)

    def pair(i):
        return (tab[i, 0], tab[i, 1])

    def forward(s, carry):
        pltpu.make_async_copy(win.at[s], win.at[s], b_recv.at[s]).wait()
        psi = wave[...]
        psis[s] = psi
        wave[...] = complex_mul(psi, window(s))

        @pl.when(s < 7)
        def _():
            wave[...] = sandwich(wave[...], pair(0), pair(1))

        return carry

    def residual():
        far_field = sandwich(wave[...], pair(2), pair(3))
        far_re, far_im = far_field[:, :WIN], far_field[:, WIN:]
        live = jnp.where(core < counts[0], 1.0, 0.0).astype(F32)
        excess = (far_re * far_re + far_im * far_im - inten[...]) * live
        wave[...] = sandwich(jnp.concatenate([excess * far_re, -(excess * far_im)], 1), pair(2), pair(4))

    def backward(n, carry):
        s = 7 - n
        u = wave[...]
        g = complex_mul(psis[s], u)
        esend[pl.ds(16 * s, 16)] = pack(g[:, :WIN].reshape(16, 8, WIN), -g[:, WIN:].reshape(16, 8, WIN))

        def send(d, carry):
            _, _, q_to, to = mate(div(d, 4), rem(d, 4))
            pltpu.make_async_remote_copy(
                src_ref=esend.at[16 * s + q_to], dst_ref=erecv.at[core, here],
                send_sem=e_send, recv_sem=e_recv, **at(s, to)
            ).start()
            return carry

        @pl.when(s != cut)
        def _():
            send(0, 0)

        @pl.when(s == cut)
        def _():
            pltpu.make_async_copy(esend.at[16 * s + q], erecv.at[core, here], e_recv).start()

        lax.fori_loop(1, 16, send, 0)

        @pl.when(s > 0)
        def _():
            wave[...] = sandwich(complex_mul(u, window(s)), pair(0), pair(1))

        return carry

    @pl.when(working)
    def _():
        lax.fori_loop(0, 8, forward, 0)
        residual()
        lax.fori_loop(0, 8, backward, 0)

    pltpu.make_async_copy(erecv, erecv, e_recv).wait()

    def place(p, sums):
        sums = list(sums)
        for j in range(2):
            in_row, in_col = masks(p, j)
            both = erecv[j, p, 0:8, :]
            scale = scale_of(erecv[j, p, 8:9, :]) * (1.0 / TOP)
            for plane in range(2):
                val = (both if plane == 0 else both << 16) >> 16
                val = val.astype(F32) * scale
                for third in range(3):
                    kept = jnp.where(in_row[third], val, 0.0)
                    for c in range(3):
                        i = (third * 3 + c) * 2 + plane
                        sums[i] = sums[i] + jnp.where(in_col[c], kept, 0.0)
        return tuple(sums)

    sums = lax.fori_loop(0, 16, place, tuple(jnp.zeros((8, WIN), F32) for _ in range(18)))
    for third in range(3):
        for c in range(3):
            re, im = sums[(third * 3 + c) * 2], sums[(third * 3 + c) * 2 + 1]
            fsend[2 * third, 8 * c : 8 * c + 8, :] = jnp.where(low, re, swap_halves(im))
            fsend[2 * third + 1, 8 * c : 8 * c + 8, :] = jnp.where(low, swap_halves(re), im)

    for d in range(1, 6):
        n_to, to = far(d)
        pltpu.make_async_remote_copy(
            src_ref=fsend.at[n_to], dst_ref=frecv.at[n_mine], send_sem=f_sem.at[0], recv_sem=f_sem.at[1], **at(cut, to)
        ).start()
    frecv[n_mine] = fsend[n_mine]

    @pl.when(working)
    def _():
        pltpu.make_async_copy(pieces.at[0:31], pieces.at[0:31], b_send).wait()
        pltpu.make_async_copy(esend.at[0:127], esend.at[0:127], e_send).wait()

    @pl.when(jnp.logical_not(working))
    def _():
        pltpu.make_async_copy(pieces, pieces, b_send).wait()

    for ref, sem in (
        (cells.at[0:5], a_sem.at[0]),
        (aux_all.at[0:15], p_sem.at[0]),
        (fsend.at[0:5], f_sem.at[0]),
        (frecv.at[0:5], f_sem.at[1]),
    ):
        pltpu.make_async_copy(ref, ref, sem).wait()
    total = frecv[0]
    for n in range(1, 6):
        total = total + frecv[n]
    total = total * GRAD_SCALE
    for rr in range(4):
        for c in range(3):
            first = (3 * rr + c) * WIN
            both = [total[8 * c + 4 * plane + rr : 8 * c + 4 * plane + rr + 1] for plane in range(2)]
            out_ref[:, first : first + WIN] = jnp.concatenate(both, 0)


def body(tab, object_slices, probe_wave, intensity, positions, counts):
    hbm = pl.BlockSpec(memory_space=pltpu.HBM)
    vmem = pl.BlockSpec(memory_space=pltpu.VMEM)
    dma = pltpu.SemaphoreType.DMA
    out = pl.pallas_call(
        kernel,
        out_shape=pltpu.VMEM((2, 12 * WIN), F32),
        in_specs=[hbm] * 6,
        out_specs=vmem,
        scratch_shapes=[
            pltpu.VMEM((2, 12 * WIN), BF16),
            pltpu.VMEM((24, WIN), BF16),
            pltpu.SMEM((2, 2), jnp.int32),
            pltpu.SMEM((1,), jnp.int32),
            pltpu.VMEM((2, WIN, WIN), F32),
            pltpu.VMEM((WIN, WIN), F32),
            pltpu.VMEM((5, 2, 2 * WIN, 2 * WIN), BF16),
            pltpu.VMEM((6, 24, WIN), BF16),
            pltpu.VMEM((3, 3, 2, 8, WIN), F32),
            pltpu.VMEM((16, 4, WIN), jnp.int32),
            pltpu.VMEM((32, 16, WIN), BF16),
            pltpu.VMEM((8, 16, 16, WIN), BF16),
            pltpu.VMEM((8, WIN, 2 * WIN), F32),
            pltpu.VMEM((WIN, 2 * WIN), F32),
            pltpu.VMEM((128, 9, WIN), jnp.int32),
            pltpu.VMEM((2, 16, 9, WIN), jnp.int32),
            pltpu.VMEM((6, 24, WIN), F32),
            pltpu.VMEM((6, 24, WIN), F32),
            dma((6,)),
            pltpu.SemaphoreType.REGULAR((3,)),
            dma((2,)), dma((2,)),
            dma, dma((8,)),
            dma, dma,
            dma((2,)),
        ],
        compiler_params=pltpu.CompilerParams(
            collective_id=0, has_side_effects=True, vmem_limit_bytes=60 << 20
        ),
    )(object_slices, positions, counts, probe_wave, intensity, tab)
    return out.reshape(1, 2, 12 * WIN)


def solution(mesh):
    tab = tables()
    in_specs = (P("cuts", None, "scan"), P(), P("scan", None, None), P("scan", None), P("scan"))
    out_specs = P("cuts", None, "scan")
    return jax.shard_map(
        functools.partial(body, tab), mesh=mesh, in_specs=in_specs, out_specs=out_specs, check_vma=False
    )
```

time: 65.4 us -> 58 us (0.89)
  the two profiles are of different devices: /device:TPU:2 before, /device:TPU:1 now
where the time goes in v3:
time: 58 us; the launch traced here: 57.5 us
  Pallas kernels  56.2 us (97%)
  between operations  0.66 us (1%)
  local copies, waits for them, and re-layouts  0.6 us (1%)
    pallas_call x1, Pallas kernels, body(): pl.pallas_call(kernel, out_shape=pltpu.VMEM((2, 12 * WIN), F32), in_specs...  56.2 us

profile of v3, /device:TPU:1, one launch (start us, length us, event | category | flops | bytes accessed | tf_op | source)
XLA Modules:
  0.0 57.5 jit_solution(8175732920289364388)
XLA Ops:
  0.7 56.2 %shard_map.64 = f32[2,1536]{1,0:T(2,128)S(1)} custom-call(bf16[1,2,1536]{2,1,0:T(2,128)(2,1)} %obj_ref.1, s32[2,2]{1,0:T(2,128)} %pos_ref.1, s32[1]{0:T(128)S(6)} %copy.9.counts_ref, f32[2,128,128]{2,1,0:T(8,128)} %probe_ref.1, f32[2,128,128]{2,1,0:T(8,128)} %inten_ref.1, bf16[5,2,256,256]{3,2,1,0:T(8,128)(2,1)} %constant.2.clone.tab_ref), custom_call_target="tpu_custom_call" | custom-call | tf_op jit(solution)/shard_map/pallas_call | solution.py:426
  56.9 0.6 %copy.8 = f32[1,2,1536]{2,1,0:T(2,128)} copy(f32[1,2,1536]{2,1,0:T(2,128)S(1)} %bitcast.1) | data formatting | bytes 24576

commit v4 on v3

--- a/solution.py
+++ b/solution.py
@@ -20,8 +20,8 @@
 
 def row_order():
     rho = np.arange(WIN)
-    q, k, rr = rho // 8, (rho // 4) % 2, rho % 4
-    return 64 * k + 16 * (q // 4) + 4 * (q % 4) + rr
+    q, h, k, rr = rho // 16, (rho // 8) % 2, (rho // 4) % 2, rho % 4
+    return 64 * h + 32 * k + 16 * (q // 4) + 4 * (q % 4) + rr
 
 
 def split_table(mat):
@@ -84,7 +84,13 @@
     shape = (WIN, WIN)
     rho = lax.broadcasted_iota(jnp.int32, shape, 0)
     lane = lax.broadcasted_iota(jnp.int32, shape, 1)
-    t = 64 * ((rho >> 2) & 1) + 16 * ((rho >> 5) & 3) + 4 * ((rho >> 3) & 3) + (rho & 3)
+    t = (
+        64 * ((rho >> 3) & 1)
+        + 32 * ((rho >> 2) & 1)
+        + 16 * ((rho >> 6) & 1)
+        + 4 * ((rho >> 4) & 3)
+        + (rho & 3)
+    )
     rows = (((t - lane - row_at) & (WIN - 1)) == 0).astype(F32).astype(BF16)
     cols = (((lane - rho - col_at) & (WIN - 1)) == 0).astype(F32).astype(BF16)
     halves = []
@@ -99,10 +105,6 @@
     return jnp.concatenate(halves, 1)
 
 
-def swap_halves(x):
-    return jnp.concatenate([x[..., 4:8, :], x[..., 0:4, :]], -2)
-
-
 STEPS = 256
 TOP = 32760.0
 
@@ -111,17 +113,21 @@
     return jnp.exp(steps.astype(F32) * (np.log(2.0) / STEPS))
 
 
-def pack(re, im):
-    most = jnp.maximum(jnp.abs(re), jnp.abs(im)).reshape(4, 4, 8, WIN)
-    most = jnp.max(jnp.max(most, axis=1), axis=1, keepdims=True)
+def pack(re, im, groups):
+    def grouped(part):
+        return part.reshape(groups, -1, 8, WIN)
+
+    most = jnp.max(grouped(jnp.maximum(jnp.abs(re), jnp.abs(im))), axis=1)
+    most = jnp.max(most, axis=1, keepdims=True)
     steps = jnp.ceil(jnp.log(jnp.maximum(most, 1e-30)) * (STEPS / np.log(2.0))).astype(jnp.int32)
     factor = (TOP * scale_of(-steps))[:, None]
-    whole_re, whole_im = (
-        jnp.floor(part.reshape(4, 4, 8, WIN) * factor + 0.5).astype(jnp.int32) for part in (re, im)
-    )
-    both = ((whole_re << 16) | (whole_im & 0xFFFF)).reshape(16, 8, WIN)
-    steps = jnp.broadcast_to(steps[:, None], (4, 4, 1, WIN)).reshape(16, 1, WIN)
-    return jnp.concatenate([both, steps], 1)
+    whole_re, whole_im = (jnp.floor(grouped(part) * factor + 0.5).astype(jnp.int32) for part in (re, im))
+    return ((whole_re << 16) | (whole_im & 0xFFFF)).reshape(re.shape), steps
+
+
+def unpack(both, steps, factor):
+    scale = scale_of(steps) * (factor / TOP)
+    return (both >> 16).astype(F32) * scale, ((both << 16) >> 16).astype(F32) * scale
 
 
 def rem(a, b):
@@ -144,24 +150,24 @@
     x, core = div(cut, 2), rem(cut, 2)
     y, z = div(me, NZ), rem(me, NZ)
     z_block, z_in = div(z, 4), rem(z, 4)
-    y_block, y_in = div(y, 4), rem(y, 4)
-    bit_b = rem(3 * y_in + z_block, 4)
+    y_block, y_in = div(y, 2), rem(y, 2)
+    bit_b = rem(y_in + z_block, 2)
     q = 4 * bit_b + z_in
-    n_mine = div(me, 16)
+    n_mine = div(me, 8)
     row_base = 16 * bit_b + 4 * z_in
 
     def worker(yi, zi, j):
-        return rem(yi + zi + 2 * j, 4)
+        return rem(yi + zi + j, 2)
 
     working = x == worker(y_in, z_in, core)
 
     def far(d):
-        n = rem(n_mine + d, 6)
-        return n, 16 * n + 4 * bit_b + z_in
+        n = rem(n_mine + d, 12)
+        return n, 8 * n + 4 * bit_b + z_in
 
     def mate(dy, dz):
-        yi, zi = rem(y_in + dy, 4), rem(z_in + dz, 4)
-        return yi, zi, 4 * rem(3 * yi + z_block, 4) + zi, (4 * y_block + yi) * NZ + 4 * z_block + zi
+        yi, zi = rem(y_in + dy, 2), rem(z_in + dz, 4)
+        return yi, zi, 4 * rem(yi + z_block, 2) + zi, (2 * y_block + yi) * NZ + 4 * z_block + zi
 
     def at(cut_to, scan_to):
         return dict(device_id={"cuts": cut_to, "scan": scan_to}, device_id_type=MESH)
@@ -180,11 +186,11 @@
         load.start()
 
     barrier = pltpu.get_barrier_semaphore()
-    for d in range(1, 6):
+    for d in range(1, 12):
         pl.semaphore_signal(barrier, inc=1, **at(cut, far(d)[1]))
     for d in range(1, 4):
         pl.semaphore_signal(barrier, inc=1, **at(cut, mate(0, d)[3]))
-        pl.semaphore_signal(barrier, inc=1, **at(cut, mate(d, 0)[3]))
+    pl.semaphore_signal(barrier, inc=1, **at(cut, mate(1, 0)[3]))
     pl.semaphore_signal(barrier, inc=1, **at(sibling, me))
     for i in range(3):
         pl.semaphore_signal(barrier, inc=1, **at(chip_at(i), me))
@@ -198,12 +204,11 @@
                 first = (3 * rr + c) * WIN
                 rows.append(flat_obj[plane : plane + 1, first : first + WIN])
     obj[...] = jnp.concatenate(rows, 0).astype(BF16)
-    pl.semaphore_wait(barrier, 15)
-
-    for d in range(1, 4):
-        pl.semaphore_signal(near_sems.at[0], inc=1, **at(cut, mate(d, 0)[3]))
-
-    for d in range(1, 6):
+    pl.semaphore_wait(barrier, 19)
+
+    pl.semaphore_signal(near_sems.at[0], inc=1, **at(cut, mate(1, 0)[3]))
+
+    for d in range(1, 12):
         pltpu.make_async_remote_copy(
             src_ref=obj, dst_ref=cells.at[n_mine], send_sem=a_sem.at[0], recv_sem=a_sem.at[1], **at(cut, far(d)[1])
         ).start()
@@ -218,9 +223,9 @@
         sub == 0, pos[0, 0], jnp.where(sub == 1, pos[0, 1], jnp.where(sub == 2, pos[1, 0], pos[1, 1]))
     )
     aux_all[here] = mine[0:4]
-    pl.semaphore_wait(near_sems.at[0], 3)
+    pl.semaphore_wait(near_sems.at[0], 1)
     pl.semaphore_signal(near_sems.at[1], inc=1, **at(sibling, me))
-    for d in range(1, 16):
+    for d in range(1, 8):
         pltpu.make_async_remote_copy(
             src_ref=aux_all.at[here], dst_ref=aux_all.at[here],
             send_sem=p_sem.at[0], recv_sem=p_sem.at[1], **at(cut, mate(d // 4, d % 4)[3])
@@ -239,39 +244,40 @@
         col_at = jnp.where(core == 0, pos[0, 1], pos[1, 1])
         wave[...] = rolled_probe(probe, row_at, col_at)
 
-    pltpu.make_async_copy(aux_all.at[0:15], aux_all.at[0:15], p_sem.at[1]).wait()
+    pltpu.make_async_copy(aux_all.at[0:7], aux_all.at[0:7], p_sem.at[1]).wait()
     pl.semaphore_wait(near_sems.at[2], 3)
-    pltpu.make_async_copy(cells.at[0:5], cells.at[0:5], a_sem.at[1]).wait()
-
-    blocks = [cells[n].astype(F32) for n in range(6)]
+    pltpu.make_async_copy(cells.at[0:11], cells.at[0:11], a_sem.at[1]).wait()
+
+    blocks = [cells[n].astype(F32) for n in range(12)]
     for third in range(3):
-        for c in range(3):
-            for plane in range(2):
-                first = 8 * c + 4 * plane
-                rows = [blocks[2 * third + k][first : first + 4] for k in range(2)]
-                strips[third, c, plane] = jnp.concatenate(rows, 0)
-
-    low = sub < 4
-    row_here = 64 * (sub >> 2) + (sub & 3) + row_base
+        for h in range(2):
+            for c in range(3):
+                for plane in range(2):
+                    first = 8 * c + 4 * plane
+                    rows = [blocks[4 * third + 2 * h + k][first : first + 4] for k in range(2)]
+                    strips[third, h, c, plane] = jnp.concatenate(rows, 0)
+
+    row_here = 32 * (sub >> 2) + (sub & 3) + row_base
 
     def masks(p, j):
         a = aux_all[p, 2 * j : 2 * j + 1, :]
         b = aux_all[p, 2 * j + 1 : 2 * j + 2, :]
-        in_row = [((row_here + WIN * third - a) & -WIN) == 0 for third in range(3)]
+        in_row = [[((row_here + (WIN * third + 64 * h) - a) & -WIN) == 0 for third in range(3)] for h in range(2)]
         in_col = [((lane + WIN * c - b) & -WIN) == 0 for c in range(3)]
         return in_row, in_col
 
     def pick(p):
         for j in range(2):
             in_row, in_col = masks(p, j)
-            planes = []
+            tiles = []
             for plane in range(2):
-                cand = []
-                for third in range(3):
-                    c0, c1, c2 = (strips[third, c, plane] for c in range(3))
-                    cand.append(jnp.where(in_col[0], c0, jnp.where(in_col[1], c1, c2)))
-                planes.append(jnp.where(in_row[0], cand[0], jnp.where(in_row[1], cand[1], cand[2])))
-            pieces[2 * p + j] = jnp.concatenate(planes, 0).astype(BF16)
+                for h in range(2):
+                    cand = []
+                    for third in range(3):
+                        c0, c1, c2 = (strips[third, h, c, plane] for c in range(3))
+                        cand.append(jnp.where(in_col[0], c0, jnp.where(in_col[1], c1, c2)))
+                    tiles.append(jnp.where(in_row[h][0], cand[0], jnp.where(in_row[h][1], cand[1], cand[2])))
+            pieces[2 * p + j] = jnp.concatenate(tiles, 0).astype(BF16)
 
     def piece_send(yi, zi, j, to):
         pltpu.make_async_remote_copy(
@@ -286,7 +292,7 @@
             piece_send(yi, zi, j, to)
         return carry
 
-    lax.fori_loop(1, 16, pick_and_send, 0)
+    lax.fori_loop(1, 8, pick_and_send, 0)
     pick(here)
     piece_send(y_in, z_in, 1 - core, me)
 
@@ -300,7 +306,7 @@
 
     def window(s):
         w = win[s].astype(F32)
-        return jnp.concatenate([w[:, 0:8].reshape(WIN, WIN), w[:, 8:16].reshape(WIN, WIN)], 1)
+        return jnp.concatenate([w[:, 0:16].reshape(WIN, WIN), w[:, 16:32].reshape(WIN, WIN)], 1)
 
     def pair(i):
         return (tab[i, 0], tab[i, 1])
@@ -328,12 +334,14 @@
         s = 7 - n
         u = wave[...]
         g = complex_mul(psis[s], u)
-        esend[pl.ds(16 * s, 16)] = pack(g[:, :WIN].reshape(16, 8, WIN), -g[:, WIN:].reshape(16, 8, WIN))
+        both, steps = pack(g[:, :WIN].reshape(8, 16, WIN), -g[:, WIN:].reshape(8, 16, WIN), 4)
+        steps = jnp.broadcast_to(steps[:, None], (4, 2, 1, WIN)).reshape(8, 1, WIN)
+        esend[pl.ds(8 * s, 8)] = jnp.concatenate([both, steps], 1)
 
         def send(d, carry):
             _, _, q_to, to = mate(div(d, 4), rem(d, 4))
             pltpu.make_async_remote_copy(
-                src_ref=esend.at[16 * s + q_to], dst_ref=erecv.at[core, here],
+                src_ref=esend.at[8 * s + q_to], dst_ref=erecv.at[core, here],
                 send_sem=e_send, recv_sem=e_recv, **at(s, to)
             ).start()
             return carry
@@ -344,9 +352,9 @@
 
         @pl.when(s == cut)
         def _():
-            pltpu.make_async_copy(esend.at[16 * s + q], erecv.at[core, here], e_recv).start()
-
-        lax.fori_loop(1, 16, send, 0)
+            pltpu.make_async_copy(esend.at[8 * s + q], erecv.at[core, here], e_recv).start()
+
+        lax.fori_loop(1, 8, send, 0)
 
         @pl.when(s > 0)
         def _():
@@ -366,26 +374,26 @@
         sums = list(sums)
         for j in range(2):
             in_row, in_col = masks(p, j)
-            both = erecv[j, p, 0:8, :]
-            scale = scale_of(erecv[j, p, 8:9, :]) * (1.0 / TOP)
+            vals = unpack(erecv[j, p, 0:16, :], erecv[j, p, 16:17, :], 1.0)
             for plane in range(2):
-                val = (both if plane == 0 else both << 16) >> 16
-                val = val.astype(F32) * scale
-                for third in range(3):
-                    kept = jnp.where(in_row[third], val, 0.0)
-                    for c in range(3):
-                        i = (third * 3 + c) * 2 + plane
-                        sums[i] = sums[i] + jnp.where(in_col[c], kept, 0.0)
+                for h in range(2):
+                    val = vals[plane][8 * h : 8 * h + 8]
+                    for third in range(3):
+                        kept = jnp.where(in_row[h][third], val, 0.0)
+                        for c in range(3):
+                            i = ((third * 2 + h) * 3 + c) * 2 + plane
+                            sums[i] = sums[i] + jnp.where(in_col[c], kept, 0.0)
         return tuple(sums)
 
-    sums = lax.fori_loop(0, 16, place, tuple(jnp.zeros((8, WIN), F32) for _ in range(18)))
-    for third in range(3):
-        for c in range(3):
-            re, im = sums[(third * 3 + c) * 2], sums[(third * 3 + c) * 2 + 1]
-            fsend[2 * third, 8 * c : 8 * c + 8, :] = jnp.where(low, re, swap_halves(im))
-            fsend[2 * third + 1, 8 * c : 8 * c + 8, :] = jnp.where(low, swap_halves(re), im)
-
-    for d in range(1, 6):
+    sums = lax.fori_loop(0, 8, place, tuple(jnp.zeros((8, WIN), F32) for _ in range(36)))
+    for half in range(6):
+        re, im = (jnp.stack([sums[(half * 3 + c) * 2 + plane] for c in range(3)]) for plane in range(2))
+        both, steps = pack(re, im, 1)
+        for k in range(2):
+            rows = [both[c, 4 * k : 4 * k + 4] for c in range(3)] + [steps[0]]
+            fsend[2 * half + k] = jnp.concatenate(rows, 0)
+
+    for d in range(1, 12):
         n_to, to = far(d)
         pltpu.make_async_remote_copy(
             src_ref=fsend.at[n_to], dst_ref=frecv.at[n_mine], send_sem=f_sem.at[0], recv_sem=f_sem.at[1], **at(cut, to)
@@ -394,28 +402,28 @@
 
     @pl.when(working)
     def _():
-        pltpu.make_async_copy(pieces.at[0:31], pieces.at[0:31], b_send).wait()
-        pltpu.make_async_copy(esend.at[0:127], esend.at[0:127], e_send).wait()
+        pltpu.make_async_copy(pieces.at[0:15], pieces.at[0:15], b_send).wait()
+        pltpu.make_async_copy(esend.at[0:63], esend.at[0:63], e_send).wait()
 
     @pl.when(jnp.logical_not(working))
     def _():
         pltpu.make_async_copy(pieces, pieces, b_send).wait()
 
     for ref, sem in (
-        (cells.at[0:5], a_sem.at[0]),
-        (aux_all.at[0:15], p_sem.at[0]),
-        (fsend.at[0:5], f_sem.at[0]),
-        (frecv.at[0:5], f_sem.at[1]),
+        (cells.at[0:11], a_sem.at[0]),
+        (aux_all.at[0:7], p_sem.at[0]),
+        (fsend.at[0:11], f_sem.at[0]),
+        (frecv.at[0:11], f_sem.at[1]),
     ):
         pltpu.make_async_copy(ref, ref, sem).wait()
-    total = frecv[0]
-    for n in range(1, 6):
-        total = total + frecv[n]
-    total = total * GRAD_SCALE
+    total = [jnp.zeros((12, WIN), F32)] * 2
+    for n in range(12):
+        part = unpack(frecv[n, 0:12, :], frecv[n, 12:13, :], GRAD_SCALE)
+        total = [total[plane] + part[plane] for plane in range(2)]
     for rr in range(4):
         for c in range(3):
             first = (3 * rr + c) * WIN
-            both = [total[8 * c + 4 * plane + rr : 8 * c + 4 * plane + rr + 1] for plane in range(2)]
+            both = [total[plane][4 * c + rr : 4 * c + rr + 1] for plane in range(2)]
             out_ref[:, first : first + WIN] = jnp.concatenate(both, 0)
 
 
@@ -436,17 +444,17 @@
             pltpu.VMEM((2, WIN, WIN), F32),
             pltpu.VMEM((WIN, WIN), F32),
             pltpu.VMEM((5, 2, 2 * WIN, 2 * WIN), BF16),
-            pltpu.VMEM((6, 24, WIN), BF16),
-            pltpu.VMEM((3, 3, 2, 8, WIN), F32),
-            pltpu.VMEM((16, 4, WIN), jnp.int32),
-            pltpu.VMEM((32, 16, WIN), BF16),
-            pltpu.VMEM((8, 16, 16, WIN), BF16),
+            pltpu.VMEM((12, 24, WIN), BF16),
+            pltpu.VMEM((3, 2, 3, 2, 8, WIN), F32),
+            pltpu.VMEM((8, 4, WIN), jnp.int32),
+            pltpu.VMEM((16, 32, WIN), BF16),
+            pltpu.VMEM((8, 8, 32, WIN), BF16),
             pltpu.VMEM((8, WIN, 2 * WIN), F32),
             pltpu.VMEM((WIN, 2 * WIN), F32),
-            pltpu.VMEM((128, 9, WIN), jnp.int32),
-            pltpu.VMEM((2, 16, 9, WIN), jnp.int32),
-            pltpu.VMEM((6, 24, WIN), F32),
-            pltpu.VMEM((6, 24, WIN), F32),
+            pltpu.VMEM((64, 17, WIN), jnp.int32),
+            pltpu.VMEM((2, 8, 17, WIN), jnp.int32),
+            pltpu.VMEM((12, 13, WIN), jnp.int32),
+            pltpu.VMEM((12, 13, WIN), jnp.int32),
             dma((6,)),
             pltpu.SemaphoreType.REGULAR((3,)),
             dma((2,)), dma((2,)),

time: 58 us -> 55.3 us (0.953)
  Pallas kernels: 56.2 us -> 53.9 us
    pallas_call x1, Pallas kernels: 56.2 us -> 53.9 us  [body(): pl.pallas_call(kernel, out_shape=pltpu.VMEM((2, 12 * WIN), F32), in_specs...]
where the time goes in v4:
time: 55.3 us; the launch traced here: 55.1 us
  Pallas kernels  53.9 us (97%)
  between operations  0.66 us (1%)
  local copies, waits for them, and re-layouts  0.6 us (1%)
    pallas_call x1, Pallas kernels, body(): pl.pallas_call(kernel, out_shape=pltpu.VMEM((2, 12 * WIN), F32), in_specs...  53.9 us

profile of v4, /device:TPU:1, one launch (start us, length us, event | category | flops | bytes accessed | tf_op | source)
XLA Modules:
  0.0 55.1 jit_solution(945427842803735209)
XLA Ops:
  0.7 53.9 %shard_map.64 = f32[2,1536]{1,0:T(2,128)S(1)} custom-call(bf16[1,2,1536]{2,1,0:T(2,128)(2,1)} %obj_ref.1, s32[2,2]{1,0:T(2,128)} %pos_ref.1, s32[1]{0:T(128)S(6)} %copy.9.counts_ref, f32[2,128,128]{2,1,0:T(8,128)} %probe_ref.1, f32[2,128,128]{2,1,0:T(8,128)} %inten_ref.1, bf16[5,2,256,256]{3,2,1,0:T(8,128)(2,1)} %constant.2.clone.tab_ref), custom_call_target="tpu_custom_call" | custom-call | tf_op jit(solution)/shard_map/pallas_call | solution.py:434
  54.5 0.6 %copy.8 = f32[1,2,1536]{2,1,0:T(2,128)} copy(f32[1,2,1536]{2,1,0:T(2,128)S(1)} %bitcast.1) | data formatting | bytes 24576

commit v5 on v4

--- a/solution.py
+++ b/solution.py
@@ -13,6 +13,7 @@
 FRESNEL = 0.5
 GRAD_SCALE = 0.25
 NZ = 12
+FARTHEST = (5, 7, 4, 8, 2, 10, 1, 11, 6, 3, 9)
 F32 = jnp.float32
 BF16 = jnp.bfloat16
 MESH = pl.DeviceIdType.MESH
@@ -169,6 +170,18 @@
         yi, zi = rem(y_in + dy, 2), rem(z_in + dz, 4)
         return yi, zi, 4 * rem(yi + z_block, 2) + zi, (2 * y_block + yi) * NZ + 4 * z_block + zi
 
+    def near(i):
+        flag = lambda hit: jnp.asarray(hit).astype(jnp.int32)
+        i = jnp.asarray(i, jnp.int32)
+        other_row, same_column = flag(i < 3) + flag(i == 6), flag(i == 6)
+        up = rem(i, 3)
+        down = 3 - up
+        upper = flag(z_in >= 2)
+        column = upper * (up + flag(up >= z_in)) + (1 - upper) * (down - flag(down <= z_in))
+        zi = same_column * z_in + (1 - same_column) * column
+        yi = other_row * (1 - y_in) + (1 - other_row) * y_in
+        return yi, zi, 4 * rem(yi + z_block, 2) + zi, (2 * y_block + yi) * NZ + 4 * z_block + zi
+
     def at(cut_to, scan_to):
         return dict(device_id={"cuts": cut_to, "scan": scan_to}, device_id_type=MESH)
 
@@ -186,7 +199,7 @@
         load.start()
 
     barrier = pltpu.get_barrier_semaphore()
-    for d in range(1, 12):
+    for d in FARTHEST:
         pl.semaphore_signal(barrier, inc=1, **at(cut, far(d)[1]))
     for d in range(1, 4):
         pl.semaphore_signal(barrier, inc=1, **at(cut, mate(0, d)[3]))
@@ -208,7 +221,7 @@
 
     pl.semaphore_signal(near_sems.at[0], inc=1, **at(cut, mate(1, 0)[3]))
 
-    for d in range(1, 12):
+    for d in FARTHEST:
         pltpu.make_async_remote_copy(
             src_ref=obj, dst_ref=cells.at[n_mine], send_sem=a_sem.at[0], recv_sem=a_sem.at[1], **at(cut, far(d)[1])
         ).start()
@@ -225,10 +238,10 @@
     aux_all[here] = mine[0:4]
     pl.semaphore_wait(near_sems.at[0], 1)
     pl.semaphore_signal(near_sems.at[1], inc=1, **at(sibling, me))
-    for d in range(1, 8):
+    for i in range(7):
         pltpu.make_async_remote_copy(
             src_ref=aux_all.at[here], dst_ref=aux_all.at[here],
-            send_sem=p_sem.at[0], recv_sem=p_sem.at[1], **at(cut, mate(d // 4, d % 4)[3])
+            send_sem=p_sem.at[0], recv_sem=p_sem.at[1], **at(cut, near(i)[3])
         ).start()
     pl.semaphore_wait(near_sems.at[1], 1)
     for i in range(3):
@@ -285,14 +298,14 @@
             send_sem=b_send, recv_sem=b_recv.at[cut], **at(2 * worker(yi, zi, j) + j, to)
         ).start()
 
-    def pick_and_send(d, carry):
-        yi, zi, _, to = mate(div(d, 4), rem(d, 4))
+    def pick_and_send(i, carry):
+        yi, zi, _, to = near(i)
         pick(4 * yi + zi)
         for j in range(2):
             piece_send(yi, zi, j, to)
         return carry
 
-    lax.fori_loop(1, 8, pick_and_send, 0)
+    lax.fori_loop(0, 7, pick_and_send, 0)
     pick(here)
     piece_send(y_in, z_in, 1 - core, me)
 
@@ -311,62 +324,61 @@
     def pair(i):
         return (tab[i, 0], tab[i, 1])
 
-    def forward(s, carry):
+    def arrive(s):
         pltpu.make_async_copy(win.at[s], win.at[s], b_recv.at[s]).wait()
         psi = wave[...]
         psis[s] = psi
-        wave[...] = complex_mul(psi, window(s))
-
-        @pl.when(s < 7)
-        def _():
-            wave[...] = sandwich(wave[...], pair(0), pair(1))
-
+        return complex_mul(psi, window(s))
+
+    def forward(s, carry):
+        wave[...] = sandwich(arrive(s), pair(0), pair(1))
         return carry
 
-    def residual():
-        far_field = sandwich(wave[...], pair(2), pair(3))
+    def residual(last):
+        far_field = sandwich(last, pair(2), pair(3))
         far_re, far_im = far_field[:, :WIN], far_field[:, WIN:]
         live = jnp.where(core < counts[0], 1.0, 0.0).astype(F32)
         excess = (far_re * far_re + far_im * far_im - inten[...]) * live
         wave[...] = sandwich(jnp.concatenate([excess * far_re, -(excess * far_im)], 1), pair(2), pair(4))
 
-    def backward(n, carry):
-        s = 7 - n
-        u = wave[...]
+    def send_gradient(s, u):
         g = complex_mul(psis[s], u)
         both, steps = pack(g[:, :WIN].reshape(8, 16, WIN), -g[:, WIN:].reshape(8, 16, WIN), 4)
         steps = jnp.broadcast_to(steps[:, None], (4, 2, 1, WIN)).reshape(8, 1, WIN)
         esend[pl.ds(8 * s, 8)] = jnp.concatenate([both, steps], 1)
-
-        def send(d, carry):
-            _, _, q_to, to = mate(div(d, 4), rem(d, 4))
-            pltpu.make_async_remote_copy(
-                src_ref=esend.at[8 * s + q_to], dst_ref=erecv.at[core, here],
-                send_sem=e_send, recv_sem=e_recv, **at(s, to)
-            ).start()
-            return carry
-
+        for i in range(7):
+            send_one(s, *near(i)[2:])
+
+    def send_one(s, q_to, to):
+        pltpu.make_async_remote_copy(
+            src_ref=esend.at[8 * s + q_to], dst_ref=erecv.at[core, here],
+            send_sem=e_send, recv_sem=e_recv, **at(s, to)
+        ).start()
+
+    def send_own(s):
         @pl.when(s != cut)
         def _():
-            send(0, 0)
+            send_one(s, q, me)
 
         @pl.when(s == cut)
         def _():
             pltpu.make_async_copy(esend.at[8 * s + q], erecv.at[core, here], e_recv).start()
 
-        lax.fori_loop(1, 8, send, 0)
-
-        @pl.when(s > 0)
-        def _():
-            wave[...] = sandwich(complex_mul(u, window(s)), pair(0), pair(1))
-
+    def backward(n, carry):
+        s = 7 - n
+        u = wave[...]
+        send_gradient(s, u)
+        wave[...] = sandwich(complex_mul(u, window(s)), pair(0), pair(1))
+        send_own(s)
         return carry
 
     @pl.when(working)
     def _():
-        lax.fori_loop(0, 8, forward, 0)
-        residual()
-        lax.fori_loop(0, 8, backward, 0)
+        lax.fori_loop(0, 7, forward, 0)
+        residual(arrive(7))
+        lax.fori_loop(0, 7, backward, 0)
+        send_gradient(0, wave[...])
+        send_own(0)
 
     pltpu.make_async_copy(erecv, erecv, e_recv).wait()
 
@@ -393,7 +405,7 @@
             rows = [both[c, 4 * k : 4 * k + 4] for c in range(3)] + [steps[0]]
             fsend[2 * half + k] = jnp.concatenate(rows, 0)
 
-    for d in range(1, 12):
+    for d in FARTHEST:
         n_to, to = far(d)
         pltpu.make_async_remote_copy(
             src_ref=fsend.at[n_to], dst_ref=frecv.at[n_mine], send_sem=f_sem.at[0], recv_sem=f_sem.at[1], **at(cut, to)

time: 55.3 us -> 53.8 us (0.973)
  Pallas kernels: 53.9 us -> 52.4 us
    pallas_call x1, Pallas kernels: 53.9 us -> 52.4 us  [body(): pl.pallas_call(kernel, out_shape=pltpu.VMEM((2, 12 * WIN), F32), in_specs...]
where the time goes in v5:
time: 53.8 us; the launch traced here: 53.7 us
  Pallas kernels  52.4 us (97%)
  between operations  0.66 us (1%)
  local copies, waits for them, and re-layouts  0.6 us (1%)
    pallas_call x1, Pallas kernels, body(): pl.pallas_call(kernel, out_shape=pltpu.VMEM((2, 12 * WIN), F32), in_specs...  52.4 us

profile of v5, /device:TPU:1, one launch (start us, length us, event | category | flops | bytes accessed | tf_op | source)
XLA Modules:
  0.0 53.7 jit_solution(15711073185625696318)
XLA Ops:
  0.7 52.4 %shard_map.64 = f32[2,1536]{1,0:T(2,128)S(1)} custom-call(bf16[1,2,1536]{2,1,0:T(2,128)(2,1)} %obj_ref.1, s32[2,2]{1,0:T(2,128)} %pos_ref.1, s32[1]{0:T(128)S(6)} %copy.9.counts_ref, f32[2,128,128]{2,1,0:T(8,128)} %probe_ref.1, f32[2,128,128]{2,1,0:T(8,128)} %inten_ref.1, bf16[5,2,256,256]{3,2,1,0:T(8,128)(2,1)} %constant.2.clone.tab_ref), custom_call_target="tpu_custom_call" | custom-call | tf_op jit(solution)/shard_map/pallas_call | solution.py:446
  53.1 0.6 %copy.8 = f32[1,2,1536]{2,1,0:T(2,128)} copy(f32[1,2,1536]{2,1,0:T(2,128)S(1)} %bitcast.1) | data formatting | bytes 24576

commit v6 on v5

--- a/solution.py
+++ b/solution.py
@@ -302,10 +302,17 @@
         yi, zi, _, to = near(i)
         pick(4 * yi + zi)
         for j in range(2):
-            piece_send(yi, zi, j, to)
+            pl.when(worker(yi, zi, j) != x)(functools.partial(piece_send, yi, zi, j, to))
         return carry
 
+    def send_here(i, carry):
+        yi, zi, _, to = near(i)
+        for j in range(2):
+            pl.when(worker(yi, zi, j) == x)(functools.partial(piece_send, yi, zi, j, to))
+        return carry
+
     lax.fori_loop(0, 7, pick_and_send, 0)
+    lax.fori_loop(0, 7, send_here, 0)
     pick(here)
     piece_send(y_in, z_in, 1 - core, me)
 
@@ -382,34 +389,38 @@
 
     pltpu.make_async_copy(erecv, erecv, e_recv).wait()
 
-    def place(p, sums):
+    def place(h, p, sums):
         sums = list(sums)
         for j in range(2):
             in_row, in_col = masks(p, j)
-            vals = unpack(erecv[j, p, 0:16, :], erecv[j, p, 16:17, :], 1.0)
+            vals = unpack(erecv[j, p, 8 * h : 8 * h + 8, :], erecv[j, p, 16:17, :], 1.0)
             for plane in range(2):
-                for h in range(2):
-                    val = vals[plane][8 * h : 8 * h + 8]
-                    for third in range(3):
-                        kept = jnp.where(in_row[h][third], val, 0.0)
-                        for c in range(3):
-                            i = ((third * 2 + h) * 3 + c) * 2 + plane
-                            sums[i] = sums[i] + jnp.where(in_col[c], kept, 0.0)
+                for third in range(3):
+                    kept = jnp.where(in_row[h][third], vals[plane], 0.0)
+                    for c in range(3):
+                        i = (third * 3 + c) * 2 + plane
+                        sums[i] = sums[i] + jnp.where(in_col[c], kept, 0.0)
         return tuple(sums)
 
-    sums = lax.fori_loop(0, 8, place, tuple(jnp.zeros((8, WIN), F32) for _ in range(36)))
-    for half in range(6):
-        re, im = (jnp.stack([sums[(half * 3 + c) * 2 + plane] for c in range(3)]) for plane in range(2))
-        both, steps = pack(re, im, 1)
-        for k in range(2):
-            rows = [both[c, 4 * k : 4 * k + 4] for c in range(3)] + [steps[0]]
-            fsend[2 * half + k] = jnp.concatenate(rows, 0)
-
-    for d in FARTHEST:
-        n_to, to = far(d)
+    def send_sum(n_to):
         pltpu.make_async_remote_copy(
-            src_ref=fsend.at[n_to], dst_ref=frecv.at[n_mine], send_sem=f_sem.at[0], recv_sem=f_sem.at[1], **at(cut, to)
+            src_ref=fsend.at[n_to], dst_ref=frecv.at[n_mine], send_sem=f_sem.at[0], recv_sem=f_sem.at[1],
+            **at(cut, 8 * n_to + 4 * bit_b + z_in)
         ).start()
+
+    for h in range(2):
+        sums = tuple(jnp.zeros((8, WIN), F32) for _ in range(18))
+        sums = lax.fori_loop(0, 8, functools.partial(place, h), sums)
+        for third in range(3):
+            re, im = (jnp.stack([sums[(third * 3 + c) * 2 + plane] for c in range(3)]) for plane in range(2))
+            both, steps = pack(re, im, 1)
+            for k in range(2):
+                rows = [both[c, 4 * k : 4 * k + 4] for c in range(3)] + [steps[0]]
+                fsend[4 * third + 2 * h + k] = jnp.concatenate(rows, 0)
+        for third in range(3):
+            for k in range(2):
+                n_to = 4 * third + 2 * h + k
+                pl.when(n_to != n_mine)(functools.partial(send_sum, n_to))
     frecv[n_mine] = fsend[n_mine]
 
     @pl.when(working)

time: 53.8 us -> 53.5 us (level)
  no operation moved by 1% of the time
where the time goes in v6:
time: 53.5 us; the launch traced here: 53.3 us
  Pallas kernels  52 us (97%)
  between operations  0.66 us (1%)
  local copies, waits for them, and re-layouts  0.6 us (1%)
    pallas_call x1, Pallas kernels, body(): pl.pallas_call(kernel, out_shape=pltpu.VMEM((2, 12 * WIN), F32), in_specs...  52 us

profile of v6, /device:TPU:1, one launch (start us, length us, event | category | flops | bytes accessed | tf_op | source)
XLA Modules:
  0.0 53.3 jit_solution(12115313295083552335)
XLA Ops:
  0.7 52.0 %shard_map.64 = f32[2,1536]{1,0:T(2,128)S(1)} custom-call(bf16[1,2,1536]{2,1,0:T(2,128)(2,1)} %obj_ref.1, s32[2,2]{1,0:T(2,128)} %pos_ref.1, s32[1]{0:T(128)S(6)} %copy.9.counts_ref, f32[2,128,128]{2,1,0:T(8,128)} %probe_ref.1, f32[2,128,128]{2,1,0:T(8,128)} %inten_ref.1, bf16[5,2,256,256]{3,2,1,0:T(8,128)(2,1)} %constant.2.clone.tab_ref), custom_call_target="tpu_custom_call" | custom-call | tf_op jit(solution)/shard_map/pallas_call | solution.py:457
  52.7 0.6 %copy.8 = f32[1,2,1536]{2,1,0:T(2,128)} copy(f32[1,2,1536]{2,1,0:T(2,128)S(1)} %bitcast.1) | data formatting | bytes 24576

commit v7 on v6

--- a/solution.py
+++ b/solution.py
@@ -216,7 +216,7 @@
             for rr in range(4):
                 first = (3 * rr + c) * WIN
                 rows.append(flat_obj[plane : plane + 1, first : first + WIN])
-    obj[...] = jnp.concatenate(rows, 0).astype(BF16)
+    obj[...] = jnp.concatenate(rows + [jnp.zeros((8, WIN), F32)], 0).astype(BF16)
     pl.semaphore_wait(barrier, 19)
 
     pl.semaphore_signal(near_sems.at[0], inc=1, **at(cut, mate(1, 0)[3]))
@@ -461,13 +461,13 @@
         out_specs=vmem,
         scratch_shapes=[
             pltpu.VMEM((2, 12 * WIN), BF16),
-            pltpu.VMEM((24, WIN), BF16),
+            pltpu.VMEM((32, WIN), BF16),
             pltpu.SMEM((2, 2), jnp.int32),
             pltpu.SMEM((1,), jnp.int32),
             pltpu.VMEM((2, WIN, WIN), F32),
             pltpu.VMEM((WIN, WIN), F32),
             pltpu.VMEM((5, 2, 2 * WIN, 2 * WIN), BF16),
-            pltpu.VMEM((12, 24, WIN), BF16),
+            pltpu.VMEM((12, 32, WIN), BF16),
             pltpu.VMEM((3, 2, 3, 2, 8, WIN), F32),
             pltpu.VMEM((8, 4, WIN), jnp.int32),
             pltpu.VMEM((16, 32, WIN), BF16),

time: 53.5 us -> 53.8 us (level)
  no operation moved by 1% of the time
where the time goes in v7:
time: 53.8 us; the launch traced here: 53.6 us
  Pallas kernels  52.4 us (97%)
  between operations  0.66 us (1%)
  local copies, waits for them, and re-layouts  0.6 us (1%)
    pallas_call x1, Pallas kernels, body(): pl.pallas_call(kernel, out_shape=pltpu.VMEM((2, 12 * WIN), F32), in_specs...  52.4 us

profile of v7, /device:TPU:1, one launch (start us, length us, event | category | flops | bytes accessed | tf_op | source)
XLA Modules:
  0.0 53.6 jit_solution(507347804960525574)
XLA Ops:
  0.7 52.4 %shard_map.64 = f32[2,1536]{1,0:T(2,128)S(1)} custom-call(bf16[1,2,1536]{2,1,0:T(2,128)(2,1)} %obj_ref.1, s32[2,2]{1,0:T(2,128)} %pos_ref.1, s32[1]{0:T(128)S(6)} %copy.9.counts_ref, f32[2,128,128]{2,1,0:T(8,128)} %probe_ref.1, f32[2,128,128]{2,1,0:T(8,128)} %inten_ref.1, bf16[5,2,256,256]{3,2,1,0:T(8,128)(2,1)} %constant.2.clone.tab_ref), custom_call_target="tpu_custom_call" | custom-call | tf_op jit(solution)/shard_map/pallas_call | solution.py:457
  53.0 0.6 %copy.8 = f32[1,2,1536]{2,1,0:T(2,128)} copy(f32[1,2,1536]{2,1,0:T(2,128)S(1)} %bitcast.1) | data formatting | bytes 24576

commit v8 on v7

--- a/solution.py
+++ b/solution.py
@@ -410,7 +410,7 @@
 
     for h in range(2):
         sums = tuple(jnp.zeros((8, WIN), F32) for _ in range(18))
-        sums = lax.fori_loop(0, 8, functools.partial(place, h), sums)
+        sums = lax.fori_loop(0, 8, functools.partial(place, h), sums, unroll=2)
         for third in range(3):
             re, im = (jnp.stack([sums[(third * 3 + c) * 2 + plane] for c in range(3)]) for plane in range(2))
             both, steps = pack(re, im, 1)

time: 53.8 us -> 53.7 us (level)
  no operation moved by 1% of the time
where the time goes in v8:
time: 53.7 us; the launch traced here: 53.6 us
  Pallas kernels  52.3 us (97%)
  between operations  0.66 us (1%)
  local copies, waits for them, and re-layouts  0.6 us (1%)
    pallas_call x1, Pallas kernels, body(): pl.pallas_call(kernel, out_shape=pltpu.VMEM((2, 12 * WIN), F32), in_specs...  52.3 us

profile of v8, /device:TPU:1, one launch (start us, length us, event | category | flops | bytes accessed | tf_op | source)
XLA Modules:
  0.0 53.6 jit_solution(7378026068320422398)
XLA Ops:
  0.7 52.3 %shard_map.64 = f32[2,1536]{1,0:T(2,128)S(1)} custom-call(bf16[1,2,1536]{2,1,0:T(2,128)(2,1)} %obj_ref.1, s32[2,2]{1,0:T(2,128)} %pos_ref.1, s32[1]{0:T(128)S(6)} %copy.9.counts_ref, f32[2,128,128]{2,1,0:T(8,128)} %probe_ref.1, f32[2,128,128]{2,1,0:T(8,128)} %inten_ref.1, bf16[5,2,256,256]{3,2,1,0:T(8,128)(2,1)} %constant.2.clone.tab_ref), custom_call_target="tpu_custom_call" | custom-call | tf_op jit(solution)/shard_map/pallas_call | solution.py:457
  53.0 0.6 %copy.8 = f32[1,2,1536]{2,1,0:T(2,128)} copy(f32[1,2,1536]{2,1,0:T(2,128)S(1)} %bitcast.1) | data formatting | bytes 24576
